TPU v7x, 32 devices: a whole 2x2x4 slice. The times are simulated.
32 devices in a mesh: seq: 8 (over z, x), chan: 4 (over y, core).
Axes of the slice: x: 2, y: 2, z: 4, core: 2. Of those that a mesh axis runs over, the one named last changes fastest.
Arguments:
- tokens: int32 [2048], P('seq'), may hold values from 0 to 255
- embed_table: bfloat16 [256, 2048], P(None, 'chan'), may hold values from -6 to 6
- short_conv: float32 [3, 2048], P(None, 'chan'), may hold values from -4 to 4
- query_branch: bfloat16 [2048, 2048], P('seq', 'chan'), may hold values from -6 to 6
- key_branch: bfloat16 [2048, 2048], P('seq', 'chan'), may hold values from -6 to 6
- decay_rate: float32 [2048], P('chan'), may hold values from 4.8828125e-05 to 0.1, as said below
- weight_first: float32 [33, 64], replicated, may hold values from -1 to 1
- weight_second: float32 [64, 64], replicated, may hold values from -0.75 to 0.75
- weight_third: float32 [64, 2048], P(None, 'chan'), may hold values from -0.75 to 0.75
- skip_gain: float32 [2048], P('chan'), may hold values from -4 to 4
- cotangent: bfloat16 [2048, 2048], P('seq', 'chan'), may hold values from -6 to 6
Outputs:
- operator_out: bfloat16 [2048, 2048], P('seq', 'chan')
- grad_query: bfloat16 [2048, 2048], P('seq', 'chan')
- grad_key: bfloat16 [2048, 2048], P('seq', 'chan')
- grad_embed: float32 [256, 2048], P('seq', 'chan')
- grad_short: float32 [3, 2048], P(None, 'chan')
- grad_skip: float32 [2048], P('chan')
- grad_first: float32 [33, 64], replicated
- grad_second: float32 [64, 64], replicated
- grad_third: float32 [64, 2048], P(None, 'chan')
Inputs may be any that keep to these rules, and one draw needn't show every extreme that they name: `decay_rate`: each channel's decay rate is either slow, log-uniform from 0.1 / 2048 to 2 / 2048, or fast, log-uniform from 0.02 to 0.1, clipped to the stated range.
All inputs are finite; a program needn't handle non-finite values.
Results may differ from a plain program's by a relative error of at most 0.0014.
Values sent between devices are 32-bit elements; how exact they have to be, the bound alone decides.
A program may use at most 64 MiB of HBM per device.

v0:
```python
import math

import jax
import jax.numpy as jnp
from jax import lax
from jax.sharding import PartitionSpec as P

BANDS = 16


highest = lax.Precision.HIGHEST
two_pi = 2.0 * math.pi


def from_behind(value, axis, steps):
    count = lax.axis_size(axis)
    leading, last = (max(0, -steps), min(count, count - steps))
    return lax.ppermute(value, axis, [(source, source + steps) for source in range(leading, last)])


def features(positions, length):
    frequency = 2 ** jnp.arange(BANDS, dtype=jnp.int32) + 1
    phases = positions[:, None] * frequency[None, :] % length
    angles = phases.astype(jnp.float32) * (two_pi / length)
    ramp_col = positions.astype(jnp.float32)[:, None] / length
    return jnp.concatenate([ramp_col, jnp.cos(angles), jnp.sin(angles)], axis=1)


def filter_forward(positions, length, weight_first, weight_second, weight_third, decay_rate):
    embedding = features(positions, length)
    pre_one = jnp.dot(
        embedding, weight_first, precision=highest, preferred_element_type=jnp.float32
    )
    act_one = jnp.sin(pre_one)
    pre_two = jnp.dot(act_one, weight_second, precision=highest, preferred_element_type=jnp.float32)
    act_two = jnp.sin(pre_two)
    shaped = jnp.dot(act_two, weight_third, precision=highest, preferred_element_type=jnp.float32)
    scaling = jnp.sqrt(jnp.expm1(-2.0 * decay_rate) / jnp.expm1(-2.0 * length * decay_rate))
    window = scaling[None, :] * jnp.exp(
        -decay_rate[None, :] * positions.astype(jnp.float32)[:, None]
    )
    return (shaped * window, (window, embedding, pre_one, act_one, pre_two, act_two))


def filter_head(grad_filter, saved_acts, weight_third):
    window, embedding, pre_one, act_one, pre_two, act_two = saved_acts
    grad_shaped = grad_filter * window
    grad_third = jnp.dot(
        act_two.T, grad_shaped, precision=highest, preferred_element_type=jnp.float32
    )
    grad_act_two = jnp.dot(
        grad_shaped, weight_third.T, precision=highest, preferred_element_type=jnp.float32
    )
    return (grad_third, grad_act_two)


def filter_tail(grad_act_two, saved_acts, weight_second):
    window, embedding, pre_one, act_one, pre_two, act_two = saved_acts
    grad_pre_two = grad_act_two * jnp.cos(pre_two)
    grad_second = jnp.dot(
        act_one.T, grad_pre_two, precision=highest, preferred_element_type=jnp.float32
    )
    grad_act_one = jnp.dot(
        grad_pre_two, weight_second.T, precision=highest, preferred_element_type=jnp.float32
    )
    grad_pre_one = grad_act_one * jnp.cos(pre_one)
    grad_first = jnp.dot(
        embedding.T, grad_pre_one, precision=highest, preferred_element_type=jnp.float32
    )
    return (grad_first, grad_second)


def rotation(first_index, second_index, modulus):
    phases = first_index * second_index % modulus
    angles = phases.astype(jnp.float32) * (two_pi / modulus)
    return (jnp.cos(angles), jnp.sin(angles))


def lane_forward(lane_rows, seq_count, points):
    width, length = lane_rows.shape
    depth_rows = length // seq_count
    blocks = lane_rows.reshape(width, seq_count, depth_rows)
    source_index = jnp.arange(seq_count, dtype=jnp.int32)
    lane_index = jnp.arange(2 * seq_count, dtype=jnp.int32)
    cosine_part, sine_part = rotation(lane_index[:, None], source_index[None, :], 2 * seq_count)
    small_table = jnp.concatenate([cosine_part, -sine_part], axis=0)
    product = jnp.einsum("kn,cnm->ckm", small_table, blocks, precision=highest)
    real_part = product[:, : 2 * seq_count]
    imag_part = product[:, 2 * seq_count :]
    cos_twist, sin_twist = rotation(
        lane_index[:, None], jnp.arange(depth_rows, dtype=jnp.int32)[None, :], points
    )
    turned = jnp.stack(
        [
            real_part * cos_twist + imag_part * sin_twist,
            imag_part * cos_twist - real_part * sin_twist,
        ]
    )
    grid_index = jnp.arange(depth_rows, dtype=jnp.int32)
    cos_block, sin_block = rotation(grid_index[:, None], grid_index[None, :], depth_rows)
    tables = jnp.concatenate([cos_block, sin_block], axis=1)
    both_parts = jnp.einsum("rckm,mj->rckj", turned, tables, precision=highest)
    return jnp.stack(
        [
            both_parts[0, :, :, :depth_rows] + both_parts[1, :, :, depth_rows:],
            both_parts[1, :, :, :depth_rows] - both_parts[0, :, :, depth_rows:],
        ]
    )


def lane_inverse(spectrum, seq_count, points):
    width = spectrum.shape[1]
    depth_rows = spectrum.shape[3]
    grid_index = jnp.arange(depth_rows, dtype=jnp.int32)
    cos_block, sin_block = rotation(grid_index[:, None], grid_index[None, :], depth_rows)
    tables = jnp.concatenate([cos_block, sin_block], axis=1)
    both_parts = jnp.einsum("rckm,mj->rckj", spectrum, tables, precision=highest)
    real_part = both_parts[0, :, :, :depth_rows] - both_parts[1, :, :, depth_rows:]
    imag_part = both_parts[1, :, :, :depth_rows] + both_parts[0, :, :, depth_rows:]
    lane_index = jnp.arange(2 * seq_count, dtype=jnp.int32)
    cos_twist, sin_twist = rotation(lane_index[:, None], grid_index[None, :], points)
    turned = jnp.stack(
        [
            real_part * cos_twist - imag_part * sin_twist,
            imag_part * cos_twist + real_part * sin_twist,
        ]
    )
    source_index = jnp.arange(seq_count, dtype=jnp.int32)
    cosine_part, sine_part = rotation(source_index[:, None], lane_index[None, :], 2 * seq_count)
    back_table = jnp.stack([cosine_part, -sine_part]) / points
    result_rows = jnp.einsum("rnk,rckm->cnm", back_table, turned, precision=highest)
    return result_rows.reshape(width, seq_count * depth_rows)


def pointwise(spectra):
    keyed_spec, filter_spec, grad_spec = spectra
    conv_spec = jnp.stack(
        [
            keyed_spec[0] * filter_spec[0] - keyed_spec[1] * filter_spec[1],
            keyed_spec[0] * filter_spec[1] + keyed_spec[1] * filter_spec[0],
        ]
    )
    back_spec = jnp.stack(
        [
            filter_spec[0] * grad_spec[0] + filter_spec[1] * grad_spec[1],
            filter_spec[0] * grad_spec[1] - filter_spec[1] * grad_spec[0],
        ]
    )
    shape_spec = jnp.stack(
        [
            keyed_spec[0] * grad_spec[0] + keyed_spec[1] * grad_spec[1],
            keyed_spec[0] * grad_spec[1] - keyed_spec[1] * grad_spec[0],
        ]
    )
    return (conv_spec, back_spec, shape_spec)


def per_device(
    tokens,
    embed_table,
    short_conv,
    query_branch,
    key_branch,
    decay_rate,
    weight_first,
    weight_second,
    weight_third,
    skip_gain,
    cotangent,
):
    seq_count = lax.axis_size("seq")
    seq_index = lax.axis_index("seq")
    row_count = query_branch.shape[0]
    chan_width = query_branch.shape[1]
    length = row_count * seq_count
    points = 2 * length
    inv_root = 1.0 / math.sqrt(length)
    vocab_size = embed_table.shape[0]
    earlier = from_behind(tokens[row_count - 2 :], "seq", 1)
    window_ids = jnp.concatenate([earlier, tokens])
    row_start = seq_index * row_count
    window_pos = row_start + jnp.arange(row_count + 2, dtype=jnp.int32) - 2
    present = window_pos >= 0
    vocab_ids = jnp.arange(vocab_size, dtype=jnp.int32)
    lookup = ((window_ids[:, None] == vocab_ids[None, :]) & present[:, None]).astype(jnp.bfloat16)
    embedded = jnp.dot(lookup, embed_table, preferred_element_type=jnp.float32)
    value_branch = (
        short_conv[0] * embedded[2:]
        + short_conv[1] * embedded[1:-1]
        + short_conv[2] * embedded[:-2]
    )
    key_rows = key_branch.astype(jnp.float32)
    keyed_value = key_rows * value_branch
    query_rows = query_branch.astype(jnp.float32)
    grad_out = cotangent.astype(jnp.float32)
    grad_z = grad_out * query_rows
    slice_width = chan_width // seq_count
    chan_start = seq_index * slice_width
    third_slice = lax.dynamic_slice_in_dim(weight_third, chan_start, slice_width, 1)
    rate_slice = lax.dynamic_slice_in_dim(decay_rate, chan_start, slice_width, 0)
    all_positions = jnp.arange(length, dtype=jnp.int32)
    filter_full, tail_acts = filter_forward(
        all_positions, length, weight_first, weight_second, third_slice, rate_slice
    )
    keyed_lanes, grad_lanes = (
        lax.all_to_all(keyed_value.T, "seq", split_axis=0, concat_axis=1, tiled=True),
        lax.all_to_all(grad_z.T, "seq", split_axis=0, concat_axis=1, tiled=True),
    )
    spectra = (
        lane_forward(keyed_lanes, seq_count, points),
        lane_forward(filter_full.T, seq_count, points),
        lane_forward(grad_lanes, seq_count, points),
    )
    conv_spec, back_spec, shape_spec = pointwise(spectra)
    conv_lanes = lane_inverse(conv_spec, seq_count, points)
    back_lanes = lane_inverse(back_spec, seq_count, points)
    filter_lanes = lane_inverse(shape_spec, seq_count, points)
    conv_rows, back_rows = (
        lax.all_to_all(conv_lanes, "seq", split_axis=1, concat_axis=0, tiled=True),
        lax.all_to_all(back_lanes, "seq", split_axis=1, concat_axis=0, tiled=True),
    )
    convolved = conv_rows.T
    back_keyed = back_rows.T
    third_small, act_two_part = filter_head(filter_lanes.T, tail_acts, third_slice)
    third_part = lax.dynamic_update_slice(
        jnp.zeros((third_small.shape[0], chan_width), jnp.float32),
        third_small,
        (jnp.zeros((), jnp.int32), chan_start),
    )
    inner_sum = convolved + skip_gain * keyed_value
    operator_out = (query_rows * inner_sum).astype(jnp.bfloat16)
    grad_query = (grad_out * inner_sum).astype(jnp.bfloat16)
    grad_keyed = back_keyed + skip_gain * grad_z
    grad_key = (grad_keyed * value_branch).astype(jnp.bfloat16)
    grad_value = grad_keyed * key_rows
    short_part = jnp.stack(
        [
            jnp.sum(grad_value * embedded[2 - offset : 2 - offset + row_count], axis=0)
            for offset in range(3)
        ]
    )
    skip_part = jnp.sum(grad_z * keyed_value, axis=0)
    ids_stacked = jnp.concatenate([window_ids[2:], window_ids[1:-1], window_ids[:-2]])
    live_stacked = jnp.concatenate([present[2:], present[1:-1], present[:-2]])
    weighted = jnp.concatenate([short_conv[offset] * grad_value for offset in range(3)], axis=0)
    vocab_rows = jnp.arange(vocab_size // seq_count * lax.axis_size("seq"), dtype=jnp.int32)
    matches = ((vocab_rows[:, None] == ids_stacked[None, :]) & live_stacked[None, :]).astype(
        jnp.float32
    )
    grad_embed = (
        lax.psum_scatter(
            jnp.dot(matches, weighted, precision=highest, preferred_element_type=jnp.float32),
            "seq",
            scatter_dimension=0,
            tiled=True,
        )
        * inv_root
    )
    grad_act_two = lax.psum(act_two_part, "chan")
    first_part, second_part = filter_tail(grad_act_two, tail_acts, weight_second)
    grad_short, grad_skip, grad_third, grad_first, grad_second = lax.psum(
        (short_part, skip_part, third_part, first_part, second_part), "seq"
    )
    return (
        operator_out,
        grad_query,
        grad_key,
        grad_embed,
        grad_short * inv_root,
        grad_skip * inv_root,
        grad_first * inv_root,
        grad_second * inv_root,
        grad_third * inv_root,
    )


def solution(mesh):
    in_specs = (
        P("seq"),
        P(None, "chan"),
        P(None, "chan"),
        P("seq", "chan"),
        P("seq", "chan"),
        P("chan"),
        P(),
        P(),
        P(None, "chan"),
        P("chan"),
        P("seq", "chan"),
    )
    out_specs = (
        P("seq", "chan"),
        P("seq", "chan"),
        P("seq", "chan"),
        P("seq", "chan"),
        P(None, "chan"),
        P("chan"),
        P(),
        P(),
        P(None, "chan"),
    )
    return jax.shard_map(
        per_device, mesh=mesh, in_specs=in_specs, out_specs=out_specs, check_vma=False
    )
```

profile of v0, /device:TPU:0, one launch (start us, length us, event | category | flops | bytes accessed | tf_op | source)
XLA Modules:
  0.0 301.9 jit_solution(439151916076778893)
XLA Ops:
  8.1 4.8 %collective-permute-start = (s32[2]{0:T(128)S(1)}, s32[2]{0:T(128)S(1)}, u32[]{:S(2)}, u32[]{:S(2)}) collective-permute-start(s32[2]{0:T(128)S(1)} %slice.133), channel_id=1, source_target_pairs={{0,4},{4,8},{8,12},{12,16},{16,20},{20,24},{24,28},{1,5},{5,9},{9,... | collective-permute-start | bytes 32 | tf_op jit(solution)/shard_map/ppermute | solution.py:18
  16.6 3.9 %fusion.147 = (f32[2048,64]{0,1:T(8,128)S(1)}, f32[2048,64]{0,1:T(8,128)}) fusion(f32[33,64]{1,0:T(8,128)} %param.17, f32[2048,16]{0,1:T(8,128)S(1)} %get-tuple-element.73, f32[2048,16]{0,1:T(8,128)S(1)} %get-tuple-element.72, f32[2048,1]{0,1:T(1,128)S(1)} %convert_multiply_fusion.5), kind=kOutput, calls=%fused_computation.237 | convolution fusion | flops 52039680 | bytes 1327360 | tf_op jit(solution)/shard_map/dot_general | solution.py:31
  23.8 4.9 %all-to-all-start.2 = ((f32[8,64,256]{2,1,0:T(8,128)}), f32[8,64,256]{2,1,0:T(8,128)S(1)}, u32[]{:S(2)}, u32[]{:S(2)}) async-start(f32[8,64,256]{2,1,0:T(8,128)} %bitcast.24), calls=%async_computation.2 | async-start | bytes 1048576 | tf_op jit(solution)/shard_map/all_to_all | solution.py:207
  30.4 3.2 %fusion.148 = (f32[2048,64]{0,1:T(8,128)S(1)}, f32[2048,64]{0,1:T(8,128)}) fusion(f32[2048,64]{0,1:T(8,128)S(1)} %get-tuple-element.74, f32[64,64]{1,0:T(8,128)S(1)} %copy-done.27), kind=kOutput, calls=%fused_computation.238 | convolution fusion | flops 100663296 | bytes 1589248 | tf_op jit(solution)/shard_map/dot_general | solution.py:35
  34.4 1.5 convolution_multiply_fusion.1
  36.9 6.1 %all-to-all-done.2 = f32[8,64,256]{2,1,0:T(8,128)S(1)} async-done(((f32[8,64,256]{2,1,0:T(8,128)}), f32[8,64,256]{2,1,0:T(8,128)S(1)}, u32[]{:S(2)}, u32[]{:S(2)}) %all-to-all-start.2) | async-done | bytes 524320 | tf_op jit(solution)/shard_map/all_to_all | solution.py:207
  43.0 4.6 %all-to-all-start = ((f32[8,64,256]{2,1,0:T(8,128)}), f32[8,64,256]{2,1,0:T(8,128)}, u32[]{:S(2)}, u32[]{:S(2)}) async-start(f32[8,64,256]{2,1,0:T(8,128)} %bitcast.4), calls=%async_computation | async-start | bytes 1048576 | tf_op jit(solution)/shard_map/all_to_all | solution.py:206
  48.5 2.7 convolution_bitcast_fusion.1
  51.8 3.3 %convolution_bitcast_fusion = f32[64,32,256]{2,1,0:T(8,128)} fusion(f32[8,64,256]{2,1,0:T(8,128)S(1)} %copy-done.12, f32[16,8]{0,1:T(8,128)S(1)} %copy-done.35, f32[16,8]{0,1:T(8,128)S(1)} %copy-done.36), kind=kOutput, calls=%fused_computation.38 | convolution fusion | flops 50331904 | bytes 2622464 | tf_op jit(solution)/shard_map/kn,cnm->ckm/dot_general | solution.py:87
  55.1 6.1 %all-to-all-done = f32[8,64,256]{2,1,0:T(8,128)} async-done(((f32[8,64,256]{2,1,0:T(8,128)}), f32[8,64,256]{2,1,0:T(8,128)}, u32[]{:S(2)}, u32[]{:S(2)}) %all-to-all-start) | async-done | bytes 524320 | tf_op jit(solution)/shard_map/all_to_all | solution.py:206
  61.2 3.2 %convolution_bitcast_fusion.2 = f32[64,32,256]{2,1,0:T(8,128)S(1)} fusion(f32[8,64,256]{2,1,0:T(8,128)} %all-to-all-done, f32[16,8]{0,1:T(8,128)} %get-tuple-element.78, f32[16,8]{0,1:T(8,128)} %get-tuple-element.79), kind=kOutput, calls=%fused_computation.40 | convolution fusion | flops 50331904 | bytes 2622464 | tf_op jit(solution)/shard_map/kn,cnm->ckm/dot_general | solution.py:87
  65.2 3.8 %fusion.16 = f32[2,64,16,512]{3,2,1,0:T(8,128)S(1)} fusion(f32[1,64,16,256]{3,2,1,0:T(8,128)S(1)} %get-tuple-element.58, f32[1,64,16,256]{3,2,1,0:T(8,128)S(1)} %get-tuple-element.59, f32[256,256]{1,0:T(8,128)S(1)} %get-tuple-element.82, f32[256,256]{1,0:T(8,128)S(1)} %get-tuple-element.83), kind=kOutput, calls=%fused_computation.18 | convolution fusion | flops 3221880832 | bytes 6815744 | tf_op jit(solution)/shard_map/rckm,mj->rckj/dot_general | solution.py:102
  69.1 4.0 %fusion = f32[2,64,16,512]{3,2,1,0:T(8,128)S(1)} fusion(f32[1,64,16,256]{3,2,1,0:T(8,128)S(1)} %get-tuple-element.60, f32[1,64,16,256]{3,2,1,0:T(8,128)S(1)} %get-tuple-element.61, f32[256,256]{1,0:T(8,128)S(1)} %get-tuple-element.82, f32[256,256]{1,0:T(8,128)S(1)} %get-tuple-element.83), kind=kOutput, calls=%fused_computation.2 | convolution fusion | flops 3221880832 | bytes 6815744 | tf_op jit(solution)/shard_map/rckm,mj->rckj/dot_general | solution.py:102
  73.2 1.8 multiply_add_fusion.1
  75.0 3.8 %fusion.4 = f32[2,64,16,512]{3,2,1,0:T(8,128)S(1)} fusion(f32[1,64,16,256]{3,2,1,0:T(8,128)S(1)} %get-tuple-element.36, f32[1,64,16,256]{3,2,1,0:T(8,128)S(1)} %get-tuple-element.35, f32[256,256]{1,0:T(8,128)S(1)} %get-tuple-element.82, f32[256,256]{1,0:T(8,128)S(1)} %get-tuple-element.83), kind=kOutput, calls=%fused_computation.6 | convolution fusion | flops 3221880832 | bytes 6815744 | tf_op jit(solution)/shard_map/rckm,mj->rckj/dot_general | solution.py:102
  79.6 1.8 multiply_subtract_fusion.1
  81.3 3.7 %fusion.8 = f32[2,64,16,512]{3,2,1,0:T(8,128)S(1)} fusion(f32[1,64,16,256]{3,2,1,0:T(8,128)S(1)} %get-tuple-element.43, f32[1,64,16,256]{3,2,1,0:T(8,128)S(1)} %get-tuple-element.44, f32[256,256]{1,0:T(8,128)S(1)} %get-tuple-element.82, f32[256,256]{1,0:T(8,128)S(1)} %get-tuple-element.83), kind=kOutput, calls=%fused_computation.10 | convolution fusion | flops 3221880832 | bytes 6815744 | tf_op jit(solution)/shard_map/rckm,mj->rckj/dot_general | solution.py:117
  87.9 4.1 %all-to-all-start.1 = ((f32[64,8,256]{2,0,1:T(8,128)}), f32[64,8,256]{2,0,1:T(8,128)}, u32[]{:S(2)}, u32[]{:S(2)}) async-start(f32[64,8,256]{2,0,1:T(8,128)} %copy.40), calls=%async_computation.1 | async-start | bytes 1048576 | tf_op jit(solution)/shard_map/all_to_all | solution.py:219
  92.3 5.2 %fusion.28 = f32[2,64,16,512]{3,2,1,0:T(8,128)S(1)} fusion(f32[1,64,16,256]{3,2,1,0:T(8,128)} %get-tuple-element.41, f32[1,64,16,256]{3,2,1,0:T(8,128)} %get-tuple-element.16, f32[256,256]{1,0:T(8,128)S(1)} %get-tuple-element.82, f32[256,256]{1,0:T(8,128)S(1)} %get-tuple-element.83), kind=kOutput, calls=%fused_computation.30 | convolution fusion | flops 3221880832 | bytes 6815744 | tf_op jit(solution)/shard_map/rckm,mj->rckj/dot_general | solution.py:117
  97.6 3.7 %fusion.20 = f32[2,64,16,512]{3,2,1,0:T(8,128)S(1)} fusion(f32[1,64,16,256]{3,2,1,0:T(8,128)S(1)} %get-tuple-element.42, f32[1,64,16,256]{3,2,1,0:T(8,128)S(1)} %get-tuple-element.24, f32[256,256]{1,0:T(8,128)S(1)} %get-tuple-element.82, f32[256,256]{1,0:T(8,128)S(1)} %get-tuple-element.83), kind=kOutput, calls=%fused_computation.22 | convolution fusion | flops 3221880832 | bytes 6815744 | tf_op jit(solution)/shard_map/rckm,mj->rckj/dot_general | solution.py:117
  107.7 5.9 %all-to-all-start.3 = ((f32[64,8,256]{2,0,1:T(8,128)}), f32[64,8,256]{2,0,1:T(8,128)S(1)}, u32[]{:S(2)}, u32[]{:S(2)}) async-start(f32[64,8,256]{2,0,1:T(8,128)} %copy.44), calls=%async_computation.3 | async-start | bytes 1048576 | tf_op jit(solution)/shard_map/all_to_all | solution.py:220
  113.9 2.4 fusion.58
  117.0 63.6 %all-reduce.6.cloned.1.call-done = f32[64,512]{1,0:T(8,128)} async-done(((f32[64,512]{1,0:T(8,128)}), f32[64,512]{1,0:T(8,128)}) %all-reduce.6.cloned.1.call-update) | async-done | bytes 131088 | tf_op jit(solution)/shard_map/psum | solution.py:261
  180.6 1.6 broadcast_multiply_fusion.3
  182.2 33.4 %all-reduce.4.cloned.1.call-done = f32[2048,64]{0,1:T(8,128)} async-done(((f32[2048,64]{0,1:T(8,128)}), f32[2048,64]{0,1:T(8,128)}) %all-reduce.4.cloned.1.call-update) | async-done | bytes 524304 | tf_op jit(solution)/shard_map/psum | solution.py:259
  215.6 3.9 %fusion.78 = f32[64,64]{1,0:T(8,128)} fusion(f32[2048,64]{0,1:T(8,128)S(1)} %copy-done.4, f32[2048,64]{0,1:T(8,128)} %all-reduce.4.cloned.1.call-done, f32[2048,64]{0,1:T(8,128)S(1)} %copy-done.5), kind=kOutput, calls=%fused_computation.132 | convolution fusion | flops 100794368 | bytes 1589248 | tf_op jit(solution)/shard_map/dot_general | solution.py:60
  219.5 5.8 %convolution_multiply_fusion = f32[2048,64]{0,1:T(8,128)} fusion(f32[64,64]{1,0:T(8,128)} %param.18, f32[2048,64]{0,1:T(8,128)} %get-tuple-element.75, f32[2048,64]{0,1:T(8,128)} %all-reduce.4.cloned.1.call-done, f32[2048,64]{0,1:T(8,128)S(1)} %copy-done.5), kind=kOutput, calls=%fused_computation | convolution fusion | flops 100925440 | bytes 2113536 | tf_op jit(solution)/shard_map/dot_general | solution.py:63
  226.8 2.0 fusion.51
  229.5 1.8 fusion.36
  232.0 37.9 %all-reduce = (f32[3,512]{1,0:T(4,128)S(1)}, f32[512]{0:T(512)S(1)}, f32[33,64]{1,0:T(8,128)S(1)}, f32[64,64]{1,0:T(8,128)S(1)}) all-reduce(f32[3,512]{1,0:T(4,128)S(1)} %pad_maximum_fusion.3, f32[512]{0:T(512)S(1)} %copy-done.49, f32[33,64]{1,0:T(8,128)S(1)} %fusion.76, ...), channel_id=1, replica_groups=mesh['seq'=8,'chan'=4] {'seq'}, use_global_device_ids=true, to_apply=%region_4.5 | all-reduce | flops 8256 | bytes 66048 | tf_op jit(solution)/shard_map/psum | solution.py:261
  272.3 21.1 %reduce-scatter.2.cloned.1.call-done = f32[32,512]{1,0:T(8,128)} async-done(((f32[256,512]{1,0:T(8,128)}), f32[32,512]{1,0:T(8,128)}) %reduce-scatter.2.cloned.1.call-update) | async-done | bytes 65552 | tf_op jit(solution)/shard_map/reduce_scatter | solution.py:251
  293.4 1.5 broadcast_multiply_fusion.4
  (164 shorter events, 29.7 us)
Async XLA Ops:
  7.2 14.2 %copy-start = (bf16[256,512]{1,0:T(8,128)(2,1)S(1)}, bf16[256,512]{1,0:T(8,128)(2,1)}, u32[]{:S(2)}) copy-start(bf16[256,512]{1,0:T(8,128)(2,1)} %param.12) | copy-start | bytes 786436
  7.2 14.8 %copy-start.16 = (bf16[256,512]{1,0:T(8,128)(2,1)S(1)}, bf16[256,512]{1,0:T(8,128)(2,1)}, u32[]{:S(2)}) copy-start(bf16[256,512]{1,0:T(8,128)(2,1)} %param.21) | copy-start | bytes 786436
  7.2 14.8 %copy-start.18 = (bf16[256,512]{1,0:T(8,128)(2,1)S(1)}, bf16[256,512]{1,0:T(8,128)(2,1)}, u32[]{:S(2)}) copy-start(bf16[256,512]{1,0:T(8,128)(2,1)} %param.14) | copy-start | bytes 786436
  7.2 14.7 %copy-start.10 = (bf16[256,512]{1,0:T(8,128)(2,1)S(1)}, bf16[256,512]{1,0:T(8,128)(2,1)}, u32[]{:S(2)}) copy-start(bf16[256,512]{1,0:T(8,128)(2,1)} %param.15) | copy-start | bytes 786436
  8.1 12.5 %collective-permute-start = (s32[2]{0:T(128)S(1)}, s32[2]{0:T(128)S(1)}, u32[]{:S(2)}, u32[]{:S(2)}) collective-permute-start(s32[2]{0:T(128)S(1)} %slice.133), channel_id=1, source_target_pairs={{0,4},{4,8},{8,12},{12,16},{16,20},{20,24},{24,28},{1,5},{5,9},{9,... | collective-permute-start | bytes 32 | tf_op jit(solution)/shard_map/ppermute | solution.py:18
  13.6 8.0 %copy-start.29 = (f32[2048,1]{0,1:T(1,128)}, f32[2048,1]{0,1:T(1,128)S(1)}, u32[]{:S(2)}) copy-start(f32[2048,1]{0,1:T(1,128)S(1)} %convert_multiply_fusion.5) | copy-start | bytes 24580
  13.7 19.9 %copy-start.25 = (f32[2048]{0:T(1024)}, f32[2048]{0:T(1024)S(1)}, u32[]{:S(2)}) copy-start(f32[2048]{0:T(1024)S(1)} %iota_convert_fusion) | copy-start | bytes 24580
  15.1 6.5 %copy-start.39 = (f32[1,512]{1,0:T(1,128)}, f32[1,512]{1,0:T(1,128)S(1)}, u32[]{:S(2)}) copy-start(f32[1,512]{1,0:T(1,128)S(1)} %get-tuple-element.62) | copy-start | bytes 6148
  15.2 6.5 %copy-start.41 = (f32[1,512]{1,0:T(1,128)}, f32[1,512]{1,0:T(1,128)S(1)}, u32[]{:S(2)}) copy-start(f32[1,512]{1,0:T(1,128)S(1)} %get-tuple-element.63) | copy-start | bytes 6148
  15.2 6.5 %copy-start.43 = (f32[1,512]{1,0:T(1,128)}, f32[1,512]{1,0:T(1,128)S(1)}, u32[]{:S(2)}) copy-start(f32[1,512]{1,0:T(1,128)S(1)} %get-tuple-element.64) | copy-start | bytes 6148
  15.8 5.9 %copy-start.14 = (f32[2048,16]{0,1:T(8,128)}, f32[2048,16]{0,1:T(8,128)S(1)}, u32[]{:S(2)}) copy-start(f32[2048,16]{0,1:T(8,128)S(1)} %get-tuple-element.73) | copy-start | bytes 393220
  16.6 16.9 %copy-start.45 = (f32[64]{0:T(128)}, f32[64]{0:T(128)S(1)}, u32[]{:S(2)}) copy-start(f32[64]{0:T(128)S(1)} %get-tuple-element.67) | copy-start | bytes 772
  16.6 16.9 %copy-start.47 = (f32[64]{0:T(128)}, f32[64]{0:T(128)S(1)}, u32[]{:S(2)}) copy-start(f32[64]{0:T(128)S(1)} %get-tuple-element.68) | copy-start | bytes 772
  20.6 9.8 %copy-start.3 = (f32[2048,64]{0,1:T(8,128)}, f32[2048,64]{0,1:T(8,128)S(1)}, u32[]{:S(2)}) copy-start(f32[2048,64]{0,1:T(8,128)S(1)} %get-tuple-element.74) | copy-start | bytes 1572868
  22.8 13.0 %copy-start.8 = (f32[256,512]{1,0:T(8,128)}, f32[256,512]{1,0:T(8,128)S(1)}, u32[]{:S(2)}) copy-start(f32[256,512]{1,0:T(8,128)S(1)} %get-tuple-element.22) | copy-start | bytes 1572868
  22.8 7.5 %copy-start.27 = (f32[64,64]{1,0:T(8,128)S(1)}, f32[64,64]{1,0:T(8,128)}, u32[]{:S(2)}) copy-start(f32[64,64]{1,0:T(8,128)} %param.18) | copy-start | bytes 49156
  23.8 19.1 %all-to-all-start.2 = ((f32[8,64,256]{2,1,0:T(8,128)}), f32[8,64,256]{2,1,0:T(8,128)S(1)}, u32[]{:S(2)}, u32[]{:S(2)}) async-start(f32[8,64,256]{2,1,0:T(8,128)} %bitcast.24), calls=%async_computation.2 | async-start | bytes 1048576 | tf_op jit(solution)/shard_map/all_to_all | solution.py:207
  43.0 18.3 %all-to-all-start = ((f32[8,64,256]{2,1,0:T(8,128)}), f32[8,64,256]{2,1,0:T(8,128)}, u32[]{:S(2)}, u32[]{:S(2)}) async-start(f32[8,64,256]{2,1,0:T(8,128)} %bitcast.4), calls=%async_computation | async-start | bytes 1048576 | tf_op jit(solution)/shard_map/all_to_all | solution.py:206
  87.9 19.8 %all-to-all-start.1 = ((f32[64,8,256]{2,0,1:T(8,128)}), f32[64,8,256]{2,0,1:T(8,128)}, u32[]{:S(2)}, u32[]{:S(2)}) async-start(f32[64,8,256]{2,0,1:T(8,128)} %copy.40), calls=%async_computation.1 | async-start | bytes 1048576 | tf_op jit(solution)/shard_map/all_to_all | solution.py:219
  92.1 88.6 %all-reduce.6.cloned.1.call-start = ((), (), s32[]{:S(2)}) async-start(), calls=%async_computation.7 | async-start | bytes 262144 | tf_op jit(solution)/shard_map/psum | solution.py:261
  105.7 10.6 %copy-start.50 = (s32[256]{0:T(256)S(1)}, s32[256]{0:T(256)}, u32[]{:S(2)}) copy-start(s32[256]{0:T(256)} %param.11) | copy-start | bytes 3076
  105.8 10.6 %copy-start.52 = (s32[256]{0:T(256)S(1)}, s32[256]{0:T(256)}, u32[]{:S(2)}) copy-start(s32[256]{0:T(256)} %get-tuple-element.65) | copy-start | bytes 3076
  105.8 10.6 %copy-start.53 = (s32[256]{0:T(256)S(1)}, s32[256]{0:T(256)}, u32[]{:S(2)}) copy-start(s32[256]{0:T(256)} %get-tuple-element.66) | copy-start | bytes 3076
  105.8 109.8 %copy-start.4 = (f32[2048,64]{0,1:T(8,128)S(1)}, f32[2048,64]{0,1:T(8,128)}, u32[]{:S(2)}) copy-start(f32[2048,64]{0,1:T(8,128)} %copy-done.3) | copy-start | bytes 1572868
  105.8 109.8 %copy-start.5 = (f32[2048,64]{0,1:T(8,128)S(1)}, f32[2048,64]{0,1:T(8,128)}, u32[]{:S(2)}) copy-start(f32[2048,64]{0,1:T(8,128)} %get-tuple-element.77) | copy-start | bytes 1572868
  107.7 118.8 %all-to-all-start.3 = ((f32[64,8,256]{2,0,1:T(8,128)}), f32[64,8,256]{2,0,1:T(8,128)S(1)}, u32[]{:S(2)}, u32[]{:S(2)}) async-start(f32[64,8,256]{2,0,1:T(8,128)} %copy.44), calls=%async_computation.3 | async-start | bytes 1048576 | tf_op jit(solution)/shard_map/all_to_all | solution.py:220
  113.6 101.9 %all-reduce.4.cloned.1.call-start = ((), (), s32[]{:S(2)}) async-start(), calls=%async_computation.6 | async-start | bytes 1048576 | tf_op jit(solution)/shard_map/psum | solution.py:259
  116.3 177.1 %reduce-scatter.2.cloned.1.call-start = ((), (), s32[]{:S(2)}) async-start(), calls=%async_computation.5 | async-start | bytes 589824 | tf_op jit(solution)/shard_map/reduce_scatter | solution.py:251
  219.5 7.2 %copy-start.9 = (f32[256,512]{1,0:T(8,128)S(1)}, f32[256,512]{1,0:T(8,128)}, u32[]{:S(2)}) copy-start(f32[256,512]{1,0:T(8,128)} %copy-done.8) | copy-start | bytes 1572868
  219.5 7.2 %copy-start.17 = (bf16[256,512]{1,0:T(8,128)(2,1)S(1)}, bf16[256,512]{1,0:T(8,128)(2,1)}, u32[]{:S(2)}) copy-start(bf16[256,512]{1,0:T(8,128)(2,1)} %param.21) | copy-start | bytes 786436
  219.5 7.3 %copy-start.19 = (bf16[256,512]{1,0:T(8,128)(2,1)S(1)}, bf16[256,512]{1,0:T(8,128)(2,1)}, u32[]{:S(2)}) copy-start(bf16[256,512]{1,0:T(8,128)(2,1)} %param.14) | copy-start | bytes 786436
  229.1 65.8 %copy-start.1 = (bf16[256,512]{1,0:T(8,128)(2,1)S(1)}, bf16[256,512]{1,0:T(8,128)(2,1)}, u32[]{:S(2)}) copy-start(bf16[256,512]{1,0:T(8,128)(2,1)} %param.12) | copy-start | bytes 786436
  (31 other events, 68.1 us)
Sparse Core Ops, SparseCore 0:
  107.9 72.7 all-reduce.5
  183.1 32.4 all-reduce.3
  231.5 61.9 reduce-scatter.1
where the time goes:
time: 308 us; the launch traced here: 302 us
  waiting for transfers between devices  130 us (42%)
  matrix products  61 us (20%)
  blocking collectives  37.9 us (12%)
  starting transfers between devices  24.9 us (8%)
  other arithmetic  21.5 us (7%)
  between operations  15 us (5%)
  local copies, waits for them, and re-layouts  11.2 us (4%)
    psum x1, waiting for transfers between devices, per_device(): lax.psum((short_part, skip_part, third_part, first_part, second_part), 's...  63.6 us
    psum x1, blocking collectives, per_device(): lax.psum((short_part, skip_part, third_part, first_part, second_part), 's...  37.9 us
    psum x1, waiting for transfers between devices, per_device(): grad_act_two = lax.psum(act_two_part, 'chan')  33.4 us
    reduce_scatter x1, waiting for transfers between devices, per_device(): lax.psum_scatter(jnp.dot(matches, weighted, precision=highest, preferred_...  21.1 us
    dot_general x3, matrix products, lane_inverse(): jnp.einsum('rckm,mj->rckj', spectrum, tables, precision=highest)  12.5 us
    dot_general x3, matrix products, lane_forward(): both_parts = jnp.einsum('rckm,mj->rckj', turned, tables, precision=highest)  11.7 us
    dot_general x3, matrix products, lane_forward(): product = jnp.einsum('kn,cnm->ckm', small_table, blocks, precision=highest)  9.1 us
  transfers between devices with their start and end apart: 8, of which 5 were waited for; matrix products, arithmetic and copies ran while one was open for 18% of the time, Pallas kernels for 0%

commit v1 on v0

--- a/solution.py
+++ b/solution.py
@@ -1,8 +1,13 @@
+import functools
 import math
 
 import jax
 import jax.numpy as jnp
+import ml_dtypes
+import numpy as np
 from jax import lax
+from jax.experimental import pallas as pl
+from jax.experimental.pallas import tpu as pltpu
 from jax.sharding import PartitionSpec as P
 
 BANDS = 16
@@ -273,6 +278,528 @@
         grad_third * inv_root,
     )
 
+MESH = pl.DeviceIdType.MESH
+f32 = jnp.float32
+bf16 = jnp.bfloat16
+
+
+def table_split(table):
+    high = table.astype(ml_dtypes.bfloat16)
+    return high, (table - high.astype(np.float32)).astype(ml_dtypes.bfloat16)
+
+
+def split(value):
+    high = value.astype(bf16)
+    return high, (value - high.astype(f32)).astype(bf16)
+
+
+def dot(left, right):
+    return jnp.dot(left, right, preferred_element_type=f32)
+
+
+def dot_full(left, right, contract=((1,), (0,))):
+    return lax.dot_general(
+        left, right, (contract, ((), ())), precision=highest, preferred_element_type=f32
+    )
+
+
+def low_lanes(shape):
+    return lax.broadcasted_iota(jnp.int32, shape, len(shape) - 1) < shape[-1] // 2
+
+
+def swap(value):
+    return pltpu.roll(value, value.shape[-1] // 2, value.ndim - 1)
+
+
+def greet(devices):
+    barrier = pltpu.get_barrier_semaphore()
+    for device in devices:
+        pl.semaphore_signal(barrier, inc=1, device_id=device, device_id_type=MESH)
+    pl.semaphore_wait(barrier, len(devices))
+
+
+def pack_rows(number, query, key, cotangent, out, base):
+    lanes = out.shape[-1]
+    block = number // 2 * lanes
+    key_part = key[:, block : block + lanes].astype(f32)
+    grad_part = cotangent[:, block : block + lanes].astype(f32) * query[
+        :, block : block + lanes
+    ].astype(f32)
+    low = low_lanes(key_part.shape)
+    if number % 2 == 0:
+        packed = jnp.where(low, key_part, swap(grad_part))
+    else:
+        packed = jnp.where(low, swap(key_part), grad_part)
+    out[number, : key.shape[0]] = packed
+
+
+def send_kernel(count, tokens, query, key, cotangent, out, staged, send_sem, recv_sem, own_sem):
+    me = lax.axis_index("seq")
+    chan = lax.axis_index("chan")
+    rows = key.shape[0]
+    token_rows = tokens[...].astype(f32)
+    for number in range(count):
+        pack_rows(number, query, key, cotangent, staged, 0)
+        staged[number, rows:] = jnp.zeros((staged.shape[1] - rows, staged.shape[2]), f32)
+        staged[number, rows : rows + token_rows.shape[0]] = token_rows
+    greet([(lax.rem(me + step, count), chan) for step in range(1, count)])
+    copies = []
+    for step in range(1, count):
+        peer = lax.rem(me + step, count)
+        copies.append(
+            pltpu.make_async_remote_copy(
+                src_ref=staged.at[peer],
+                dst_ref=out.at[me],
+                send_sem=send_sem.at[step],
+                recv_sem=recv_sem.at[step],
+                device_id=(peer, chan),
+                device_id_type=MESH,
+            )
+        )
+    for copy in copies:
+        copy.start()
+    own = pltpu.make_async_copy(staged.at[me], out.at[me], own_sem)
+    own.start()
+    own.wait()
+    for copy in copies:
+        copy.wait()
+
+
+def conv_kernel(
+    count,
+    rows,
+    coefs,
+    arrived,
+    params,
+    first,
+    second,
+    feats,
+    twiddles,
+    table_high,
+    table_low,
+    pay,
+    hidden,
+    state,
+    filters,
+    total,
+    shape_total,
+    value,
+    embedded,
+    gated,
+    onehot,
+    acts,
+    windows,
+):
+    lanes = params.shape[1]
+    half = lanes // 2
+    vocab = onehot.shape[0]
+    length = count * rows
+    low = low_lanes((rows, lanes))
+    sign = jnp.where(low, 1.0, -1.0).astype(f32)
+    third = params[vocab : vocab + 64]
+    top = vocab + 64
+    rate, scale, skip = params[top : top + 1], params[top + 1 : top + 2], params[top + 2 : top + 3]
+    taps = [params[top + 3 + j : top + 4 + j] for j in range(3)]
+    table = params[:vocab].astype(bf16)
+
+    pre_one = dot_full(first[...], feats[...], ((0,), (0,)))
+    act_one = jnp.sin(pre_one)
+    acts[0] = act_one
+    acts[1] = jnp.cos(pre_one)
+    pre_two = dot_full(second[...], act_one, ((0,), (0,)))
+    acts[2] = jnp.sin(pre_two)
+    acts[3] = jnp.cos(pre_two)
+
+    embedded[:8] = jnp.zeros((8, lanes), f32)
+    row_ids = lax.broadcasted_iota(jnp.int32, (rows, lanes), 0).astype(f32)
+    vocab_ids = lax.broadcasted_iota(jnp.int32, (vocab, lanes), 0).astype(f32)
+    for block in range(count):
+        act_rows = acts[2, :, block * rows : (block + 1) * rows].T
+        window = scale * jnp.exp(-rate * (row_ids + float(block * rows)))
+        windows[block] = window
+        filters[block] = dot_full(act_rows, third) * window
+        for piece in range(rows // lanes):
+            ids = arrived[block, rows + piece : rows + piece + 1]
+            matches = jnp.where(vocab_ids == ids, 1.0, 0.0)
+            start = block * rows + piece * lanes
+            onehot[:, start : start + lanes] = matches.astype(bf16)
+            embedded[8 + start : 8 + start + lanes] = dot(matches.T.astype(bf16), table)
+    for block in range(count):
+        start = 8 + block * rows
+        branch = (
+            taps[0] * embedded[start : start + rows]
+            + taps[1] * embedded[start - 1 : start - 1 + rows]
+            + taps[2] * embedded[start - 2 : start - 2 + rows]
+        )
+        value[block] = branch
+        packed = arrived[block, :rows]
+        state[block] = jnp.where(low, packed * branch, packed)
+    total[...] = jnp.zeros_like(total)
+    shape_total[...] = jnp.zeros_like(shape_total)
+
+    def spread(both):
+        high, rest = split(both)
+        product = (
+            dot(table_high[...], high) + dot(table_high[...], rest) + dot(table_low[...], high)
+        )
+        return product[:rows], product[rows:]
+
+    def one(lane, carry):
+        cos_t = twiddles[lane, 0]
+        sin_t = twiddles[lane, 1]
+
+        def forward(ref):
+            real = jnp.zeros((rows, lanes), f32)
+            imag = jnp.zeros((rows, lanes), f32)
+            for n in range(count):
+                piece = ref[n]
+                real = real + coefs[lane, n] * piece
+                imag = imag - coefs[lane, count + n] * piece
+            turned = jnp.concatenate(
+                [real * cos_t + imag * sin_t, imag * cos_t - real * sin_t], axis=1
+            )
+            by_cos, by_sin = spread(turned)
+            return (
+                by_cos[:, :lanes] + by_sin[:, lanes:],
+                by_cos[:, lanes:] - by_sin[:, :lanes],
+            )
+
+        xr, xi = forward(state)
+        fr, fi = forward(filters)
+        fi = fi * sign
+        by_cos, by_sin = spread(jnp.concatenate([xr * fr - xi * fi, xr * fi + xi * fr], axis=1))
+        zr = by_cos[:, :lanes] - by_sin[:, lanes:]
+        zi = by_cos[:, lanes:] + by_sin[:, :lanes]
+        ur = zr * cos_t - zi * sin_t
+        ui = zr * sin_t + zi * cos_t
+        gr, gi = swap(xr), swap(xi)
+        hr = xr * gr + xi * gi
+        hi = xr * gi - xi * gr
+        by_cos, by_sin = spread(jnp.where(low, hr, swap(hi)))
+        both = by_cos - sign * swap(by_sin)
+        part_cos = both * jnp.where(low, cos_t, -sin_t)
+        part_sin = both * jnp.where(low, sin_t, cos_t)
+        for n in range(count):
+            cosine = coefs[lane, 2 * count + n]
+            sine = coefs[lane, 3 * count + n]
+            total[n] += cosine * ur - sine * ui
+            shape_total[n] += cosine * part_cos - sine * part_sin
+        return carry
+
+    lax.fori_loop(0, count + 1, one, 0)
+
+    gated[length:] = jnp.zeros((8, lanes), f32)
+    short_sums = [jnp.zeros((1, lanes), f32) for _ in range(3)]
+    skip_sum = jnp.zeros((1, lanes), f32)
+    third_sum = jnp.zeros((64, lanes), f32)
+    for block in range(count):
+        mine = state[block]
+        summed = total[block] + skip * mine
+        pay[block, :rows] = jnp.where(low, summed, summed * value[block])
+        grad_value = summed * swap(arrived[block, :rows])
+        start = block * rows
+        gated[start : start + rows] = grad_value
+        for j in range(3):
+            short_sums[j] += jnp.sum(
+                grad_value * embedded[8 + start - j : 8 + start - j + rows], axis=0, keepdims=True
+            )
+        skip_sum += jnp.sum(mine * swap(mine), axis=0, keepdims=True)
+        grad_rows = shape_total[block]
+        grad_rows = (grad_rows + swap(grad_rows)) * windows[block]
+        columns = pl.ds(start, rows)
+        third_sum += dot_full(acts[2, :, columns], grad_rows)
+        grad_act = dot_full(jnp.where(low_lanes(third.shape), third, 0.0), grad_rows, ((1,), (1,)))
+        acts[3, :, columns] = grad_act * acts[3, :, columns]
+    embed_sum = jnp.zeros((vocab, lanes), f32)
+    for block in range(count):
+        start = block * rows
+        spread_rows = (
+            taps[0] * gated[start : start + rows]
+            + taps[1] * gated[start + 1 : start + 1 + rows]
+            + taps[2] * gated[start + 2 : start + 2 + rows]
+        )
+        high, rest = split(spread_rows)
+        matches = onehot[:, start : start + rows]
+        embed_sum += dot(matches, high) + dot(matches, rest)
+    inv_root = 1.0 / math.sqrt(length)
+    grad_pre_two = acts[3]
+    grad_second = dot_full(acts[0], grad_pre_two, ((1,), (1,))) * inv_root
+    grad_pre_one = dot_full(second[...], grad_pre_two) * acts[1]
+    grad_first = dot_full(feats[...], grad_pre_one, ((1,), (1,))) * inv_root
+    hidden[:64] = grad_second
+    hidden[64:] = grad_first
+    share = vocab // count
+    small = jnp.concatenate(
+        [third_sum, *short_sums, skip_sum, jnp.zeros((4, lanes), f32)], axis=0
+    ) * inv_root
+    for block in range(count):
+        pay[block, rows : rows + share] = embed_sum[block * share : (block + 1) * share] * inv_root
+        pay[block, rows + share :] = small
+
+
+def return_kernel(
+    count,
+    groups,
+    pay,
+    hidden,
+    query,
+    cotangent,
+    out,
+    grad_query,
+    grad_key,
+    grad_embed,
+    small,
+    summed,
+    landed,
+    by_chan,
+    by_seq,
+    held,
+    send_sem,
+    recv_sem,
+    own_sem,
+    chan_send,
+    chan_recv,
+    seq_send,
+    seq_recv,
+):
+    me = lax.axis_index("seq")
+    chan = lax.axis_index("chan")
+    rows = query.shape[0]
+    lanes = pay.shape[2]
+    share = grad_embed.shape[0]
+    peers = [(lax.rem(me + step, count), chan) for step in range(1, count)]
+    across = [(me, lax.rem(chan + step, groups)) for step in range(1, groups)]
+    greet(peers + across)
+
+    def post(source, target, send, recv, device):
+        copy = pltpu.make_async_remote_copy(
+            src_ref=source,
+            dst_ref=target,
+            send_sem=send,
+            recv_sem=recv,
+            device_id=device,
+            device_id_type=MESH,
+        )
+        copy.start()
+        return copy
+
+    wide = [
+        post(hidden, by_chan.at[n], chan_send.at[n], chan_recv.at[n], device)
+        for n, device in enumerate(across)
+    ]
+    main = [
+        post(pay.at[device[0]], landed.at[me], send_sem.at[n], recv_sem.at[n], device)
+        for n, device in enumerate(peers)
+    ]
+    own = pltpu.make_async_copy(pay.at[me], landed.at[me], own_sem)
+    own.start()
+    for copy in wide:
+        copy.wait()
+    group_sum = hidden[...]
+    for n in range(groups - 1):
+        group_sum = group_sum + by_chan[n]
+    held[...] = group_sum
+    along = [
+        post(held, by_seq.at[me], seq_send.at[n], seq_recv.at[n], device)
+        for n, device in enumerate(peers)
+    ]
+    by_seq[me] = group_sum
+    own.wait()
+    for copy in main:
+        copy.wait()
+    for block in range(count // 2):
+        columns = pl.ds(block * lanes, lanes)
+        even, odd = landed[2 * block], landed[2 * block + 1]
+        low = low_lanes((rows, lanes))
+        inner = jnp.where(low, even[:rows], swap(odd[:rows]))
+        out[:, columns] = (query[:, columns].astype(f32) * inner).astype(bf16)
+        grad_query[:, columns] = (cotangent[:, columns].astype(f32) * inner).astype(bf16)
+        grad_key[:, columns] = jnp.where(low, swap(even[:rows]), odd[:rows]).astype(bf16)
+        rest_even, rest_odd = even[rows:], odd[rows:]
+        rest = jnp.where(low_lanes(rest_even.shape), swap(rest_even), rest_odd)
+        grad_embed[:, columns] = rest[:share]
+        small[:, columns] = rest[share:]
+    for copy in along:
+        copy.wait()
+    everything = by_seq[0]
+    for n in range(1, count):
+        everything = everything + by_seq[n]
+    summed[...] = everything
+
+
+def feature_table(length):
+    positions = np.arange(length, dtype=np.int64)
+    frequency = 2 ** np.arange(BANDS, dtype=np.int64) + 1
+    phases = positions[:, None] * frequency[None, :] % length
+    angles = phases.astype(np.float32) * np.float32(two_pi / length)
+    ramp = positions.astype(np.float32)[:, None] / np.float32(length)
+    return np.concatenate([ramp, np.cos(angles), np.sin(angles)], axis=1).T.astype(np.float32)
+
+
+def fused_device(
+    tokens,
+    embed_table,
+    short_conv,
+    query_branch,
+    key_branch,
+    decay_rate,
+    weight_first,
+    weight_second,
+    weight_third,
+    skip_gain,
+    cotangent,
+):
+    count = lax.axis_size("seq")
+    groups = lax.axis_size("chan")
+    seq_index = lax.axis_index("seq")
+    rows, chan_width = query_branch.shape
+    length = rows * count
+    points = 2 * length
+    vocab = embed_table.shape[0]
+    hidden_units = weight_second.shape[0]
+    feat = weight_first.shape[0]
+    slice_width = chan_width // count
+    lanes = 2 * slice_width
+    share = vocab // count
+    scaling = jnp.sqrt(jnp.expm1(-2.0 * decay_rate) / jnp.expm1(-2.0 * length * decay_rate))
+    stacked = jnp.concatenate(
+        [
+            embed_table.astype(f32),
+            weight_third,
+            decay_rate[None],
+            scaling[None],
+            skip_gain[None],
+            short_conv,
+            jnp.zeros((2, chan_width), f32),
+        ],
+        axis=0,
+    )
+    mine = lax.dynamic_slice_in_dim(stacked, seq_index * slice_width, slice_width, 1)
+    params = jnp.concatenate([mine, mine], axis=1)
+
+    vmem = pl.BlockSpec(memory_space=pltpu.VMEM)
+    smem = pl.BlockSpec(memory_space=pltpu.SMEM)
+    dma = pltpu.SemaphoreType.DMA
+    arrived_rows = rows + 8
+    arrived = pl.pallas_call(
+        functools.partial(send_kernel, count),
+        out_shape=jax.ShapeDtypeStruct((count, arrived_rows, lanes), f32),
+        in_specs=[vmem] * 4,
+        out_specs=vmem,
+        scratch_shapes=[
+            pltpu.VMEM((count, arrived_rows, lanes), f32),
+            dma((count,)),
+            dma((count,)),
+            dma(()),
+        ],
+        compiler_params=pltpu.CompilerParams(
+            collective_id=0, has_side_effects=True, vmem_limit_bytes=32 * 2**20
+        ),
+        name="send_slices",
+    )(tokens.reshape(rows // lanes, lanes), query_branch, key_branch, cotangent)
+
+    depth = np.arange(rows)
+    turns = np.arange(count + 1)
+    angle = two_pi * (depth[:, None] * depth[None, :] % rows) / rows
+    tables = np.concatenate([np.cos(angle), np.sin(angle)], axis=0).astype(np.float32)
+    table_high, table_low = table_split(tables)
+    twist = two_pi * (turns[:, None] * depth[None, :]) / points
+    twiddles = np.stack([np.cos(twist), np.sin(twist)], axis=1).astype(np.float32)
+    twiddles = jnp.broadcast_to(jnp.asarray(twiddles)[..., None], (count + 1, 2, rows, lanes))
+    small_angle = two_pi * (turns[:, None] * np.arange(count)[None, :] % (2 * count)) / (2 * count)
+    weight = np.where((turns == 0) | (turns == count), 1.0, 2.0)[:, None] / points
+    coefs = np.concatenate(
+        [
+            np.cos(small_angle),
+            np.sin(small_angle),
+            weight * np.cos(small_angle),
+            weight * np.sin(small_angle),
+        ],
+        axis=1,
+    ).astype(np.float32)
+    pay_rows = rows + share + hidden_units + 8
+    pay, hidden = pl.pallas_call(
+        functools.partial(conv_kernel, count, rows),
+        out_shape=(
+            jax.ShapeDtypeStruct((count, pay_rows, lanes), f32),
+            jax.ShapeDtypeStruct((hidden_units + feat, hidden_units), f32),
+        ),
+        in_specs=[smem] + [vmem] * 8,
+        out_specs=(vmem, vmem),
+        scratch_shapes=[
+            pltpu.VMEM((count, rows, lanes), f32),
+            pltpu.VMEM((count, rows, lanes), f32),
+            pltpu.VMEM((count, rows, lanes), f32),
+            pltpu.VMEM((count, rows, lanes), f32),
+            pltpu.VMEM((count, rows, lanes), f32),
+            pltpu.VMEM((length + 8, lanes), f32),
+            pltpu.VMEM((length + 8, lanes), f32),
+            pltpu.VMEM((vocab, length), bf16),
+            pltpu.VMEM((4, hidden_units, length), f32),
+            pltpu.VMEM((count, rows, lanes), f32),
+        ],
+        compiler_params=pltpu.CompilerParams(vmem_limit_bytes=48 * 2**20),
+        name="convolve_slices",
+    )(
+        jnp.asarray(coefs),
+        arrived,
+        params,
+        weight_first,
+        weight_second,
+        jnp.asarray(feature_table(length)),
+        twiddles,
+        jnp.asarray(table_high),
+        jnp.asarray(table_low),
+    )
+    hidden_shape = (hidden_units + feat, hidden_units)
+    out, grad_query, grad_key, grad_embed, small, summed = pl.pallas_call(
+        functools.partial(return_kernel, count, groups),
+        out_shape=(
+            jax.ShapeDtypeStruct((rows, chan_width), bf16),
+            jax.ShapeDtypeStruct((rows, chan_width), bf16),
+            jax.ShapeDtypeStruct((rows, chan_width), bf16),
+            jax.ShapeDtypeStruct((share, chan_width), f32),
+            jax.ShapeDtypeStruct((hidden_units + 8, chan_width), f32),
+            jax.ShapeDtypeStruct(hidden_shape, f32),
+        ),
+        in_specs=[vmem] * 4,
+        out_specs=(vmem,) * 6,
+        scratch_shapes=[
+            pltpu.VMEM((count, pay_rows, lanes), f32),
+            pltpu.VMEM((groups,) + hidden_shape, f32),
+            pltpu.VMEM((count,) + hidden_shape, f32),
+            pltpu.VMEM(hidden_shape, f32),
+            dma((count,)),
+            dma((count,)),
+            dma(()),
+            dma((groups,)),
+            dma((groups,)),
+            dma((count,)),
+            dma((count,)),
+        ],
+        compiler_params=pltpu.CompilerParams(
+            collective_id=1, has_side_effects=True, vmem_limit_bytes=32 * 2**20
+        ),
+        name="return_slices",
+    )(pay, hidden, query_branch, cotangent)
+    return (
+        out,
+        grad_query,
+        grad_key,
+        grad_embed,
+        small[hidden_units : hidden_units + 3],
+        small[hidden_units + 3],
+        summed[hidden_units:],
+        summed[:hidden_units],
+        small[:hidden_units],
+    )
+
+
+def per_slice(*arrays):
+    packed_width = 2 * arrays[3].shape[1] // lax.axis_size("seq")
+    body = fused_device if packed_width % 128 == 0 else per_device
+    return body(*arrays)
+
 
 def solution(mesh):
     in_specs = (
@@ -300,5 +827,5 @@
         P(None, "chan"),
     )
     return jax.shard_map(
-        per_device, mesh=mesh, in_specs=in_specs, out_specs=out_specs, check_vma=False
-    )
+        per_slice, mesh=mesh, in_specs=in_specs, out_specs=out_specs, check_vma=False
+    )

time: 308 us -> 112 us (0.36); the launches traced: 302 us -> 112 us
  waiting for transfers between devices: 130 us -> 0 us
  Pallas kernels: 0 us -> 100 us
  matrix products: 61 us -> 0 us
  blocking collectives: 37.9 us -> 0 us
  starting transfers between devices: 24.9 us -> 0 us
  other arithmetic: 21.5 us -> 0.87 us
  between operations: 15 us -> 0.83 us
    pallas_call x0 -> x3, Pallas kernels: none -> 100 us  [the longest x1 49.5 us: fused_device(): pl.pallas_call(functools.partial(return_kernel, count, groups), out_shape...]
    psum x2 -> x0, waiting for transfers between devices: 97 us -> none  [the longest x1 63.6 us: per_device(): lax.psum((short_part, skip_part, third_part, first_part, second_part), 's...]
    dot_general x22 -> x0, matrix products: 61 us -> none  [the longest x3 12.5 us: lane_inverse(): jnp.einsum('rckm,mj->rckj', spectrum, tables, precision=highest)]
    psum x1 -> x0, blocking collectives: 37.9 us -> none  [per_device(): lax.psum((short_part, skip_part, third_part, first_part, second_part), 's...]
    reduce_scatter x1 -> x0, waiting for transfers between devices: 21.1 us -> none  [per_device(): lax.psum_scatter(jnp.dot(matches, weighted, precision=highest, preferred_...]
    all_to_all x4 -> x0, starting transfers between devices: 19.5 us -> none  [the longest x1 5.89 us: per_device(): lax.all_to_all(back_lanes, 'seq', split_axis=1, concat_axis=0, tiled=True)]
    all_to_all x4 -> x0, waiting for transfers between devices: 12.2 us -> none  [the longest x1 6.12 us: per_device(): lax.all_to_all(keyed_value.T, 'seq', split_axis=0, concat_axis=1, tiled=T...]
    mul x7 -> x0, other arithmetic: 5.64 us -> none  [the longest x1 1.57 us: per_device(): grad_third * inv_root]
  transfers between devices with their start and end apart: 8 -> 0, of which waited for: 5 -> 0; matrix products, arithmetic and copies ran while one was open for 18% -> 0% of each run, Pallas kernels for 0% -> 0%
where the time goes in v1:
time: 112 us
  Pallas kernels  100 us (89%)
  local copies, waits for them, and re-layouts  9.71 us (9%)
    pallas_call x1, Pallas kernels, fused_device(): pl.pallas_call(functools.partial(return_kernel, count, groups), out_shape...  49.5 us
    pallas_call x1, Pallas kernels, fused_device(): pl.pallas_call(functools.partial(conv_kernel, count, rows), out_shape=(ja...  26.9 us
    pallas_call x1, Pallas kernels, fused_device(): pl.pallas_call(functools.partial(send_kernel, count), out_shape=jax.Shape...  23.8 us
    unnamed x26, local copies, waits for them, and re-layouts  3.18 us
    concatenate x1, local copies, waits for them, and re-layouts, fused_device(): jnp.concatenate([embed_table.astype(f32), weight_third, decay_rate[None],...  2.68 us

profile of v1, /device:TPU:0, one launch (start us, length us, event | category | flops | bytes accessed | tf_op | source)
XLA Modules:
  0.0 111.5 jit_solution(965411615699155073)
XLA Ops:
  0.6 0.0 copy-start.1
  0.7 0.0 copy-start
  0.7 0.0 copy-start.3
  0.7 0.0 copy-start.9
  0.7 0.8 fusion
  1.5 2.7 %concatenate.6 = f32[328,512]{1,0:T(8,128)S(1)} concatenate(bf16[256,512]{1,0:T(8,128)(2,1)} %param.17, f32[64,512]{1,0:T(8,128)} %param.24, f32[1,512]{1,0:T(1,128)} %bitcast.6, f32[1,512]{1,0:T(1,128)S(1)} %bitcast.7, f32[1,512]{1,0:T(1,128)} %bitcast.8, f32[3,512]{1,0:T(4,128)} %param.18, f32[2,512]{1,0:T(2,128)S(1)} %broadcast_in_dim.21), dimensions={0} | concatenate | bytes 1081344 | tf_op jit(solution)/shard_map/concatenate | solution.py:665
  4.1 0.0 copy-start.10
  4.2 0.1 constant_dynamic-slice_fusion
  4.3 0.1 pad_maximum_fusion.params
  4.4 23.8 %send_slices.1.arrived = f32[8,264,128]{2,1,0:T(8,128)S(1)} custom-call(s32[2,128]{1,0:T(2,128)S(1)} %bitcast.5, bf16[256,512]{1,0:T(8,128)(2,1)S(1)} %copy-done, bf16[256,512]{1,0:T(8,128)(2,1)S(1)} %copy-done.3, bf16[256,512]{1,0:T(8,128)(2,1)S(1)} %copy-done.1), custom_call_target="tpu_custom_call" | custom-call | tf_op jit(solution)/shard_map/send_slices/pallas_call | solution.py:684
  28.2 0.0 copy-done.10
  28.2 0.0 copy-start.2
  28.2 0.0 copy-start.4
  28.3 0.0 copy-start.5
  28.3 0.0 copy-start.6
  28.3 0.0 copy-start.7
  28.3 0.0 copy-start.8
  28.3 0.7 broadcast_in_dim.22.twiddles
  29.0 0.2 copy-done.2
  29.2 0.1 copy-done.4
  29.3 0.1 copy-done.5
  29.4 26.9 %convolve_slices.1 = (f32[8,360,128]{2,1,0:T(8,128)S(1)}, f32[97,64]{1,0:T(8,128)S(1)}) custom-call(f32[9,32]{1,0:T(8,128)S(1)} %copy-done.8, f32[8,264,128]{2,1,0:T(8,128)S(1)} %send_slices.1.arrived, f32[328,128]{1,0:T(8,128)S(1)} %pad_maximum_fusion.params, f32[33,64]{1,0:T(8,128)S(1)} %copy-done.7, f32[64,64]{1,0:T(8,128)S(1)} %copy-done.6, ...), custom_call_target="tpu_custom_call" | custom-call | tf_op jit(solution)/shard_map/convolve_slices/pallas_call | solution.py:721
  56.2 49.5 %return_slices.1 = (bf16[256,512]{1,0:T(8,128)(2,1)S(1)}, bf16[256,512]{1,0:T(8,128)(2,1)S(1)}, bf16[256,512]{1,0:T(8,128)(2,1)S(1)}, f32[32,512]{1,0:T(8,128)S(...) custom-call(f32[8,360,128]{2,1,0:T(8,128)S(1)} %get-tuple-element.17.pay, f32[97,64]{1,0:T(8,128)S(1)} %get-tuple-element.18.hidden, ...), custom_call_target="tpu_custom_call" | custom-call | tf_op jit(solution)/shard_map/return_slices/pallas_call | solution.py:755
  105.7 0.6 slice.16
  106.3 0.6 slice.15
  106.9 0.7 slice.19
  107.5 0.6 slice.17
  108.1 0.6 slice.18
  108.8 0.7 copy.29
  109.5 0.7 copy.30
  110.2 0.7 copy.31
  110.9 0.6 copy.32
  (8 shorter events, 0.0 us)
Async XLA Ops:
  0.6 3.8 %copy-start.1 = (bf16[256,512]{1,0:T(8,128)(2,1)S(1)}, bf16[256,512]{1,0:T(8,128)(2,1)}, u32[]{:S(2)}) copy-start(bf16[256,512]{1,0:T(8,128)(2,1)} %cotangent.3) | copy-start | bytes 786436
  0.7 3.8 %copy-start = (bf16[256,512]{1,0:T(8,128)(2,1)S(1)}, bf16[256,512]{1,0:T(8,128)(2,1)}, u32[]{:S(2)}) copy-start(bf16[256,512]{1,0:T(8,128)(2,1)} %query.3) | copy-start | bytes 786436
  0.7 3.8 %copy-start.3 = (bf16[256,512]{1,0:T(8,128)(2,1)S(1)}, bf16[256,512]{1,0:T(8,128)(2,1)}, u32[]{:S(2)}) copy-start(bf16[256,512]{1,0:T(8,128)(2,1)} %key.1) | copy-start | bytes 786436
  0.7 3.8 %copy-start.9 = (s32[256]{0:T(256)S(1)}, s32[256]{0:T(256)}, u32[]{:S(2)}) copy-start(s32[256]{0:T(256)} %param.16) | copy-start | bytes 3076
  4.1 24.1 %copy-start.10 = (f32[9,2,256]{2,1,0:T(2,128)S(1)}, f32[9,2,256]{2,1,0:T(2,128)}, u32[]{:S(2)}) copy-start(f32[9,2,256]{2,1,0:T(2,128)} %constant.28.clone) | copy-start | bytes 55300
  28.2 1.0 copy-start.2
  28.2 1.0 copy-start.4
  28.3 1.1 copy-start.5
  28.3 1.1 copy-start.6
  28.3 1.1 copy-start.7
  28.3 1.1 copy-start.8

commit v2 on v0

--- a/solution.py
+++ b/solution.py
@@ -1,8 +1,13 @@
+import functools
 import math
 
 import jax
 import jax.numpy as jnp
+import ml_dtypes
+import numpy as np
 from jax import lax
+from jax.experimental import pallas as pl
+from jax.experimental.pallas import tpu as pltpu
 from jax.sharding import PartitionSpec as P
 
 BANDS = 16
@@ -273,6 +278,595 @@
         grad_third * inv_root,
     )
 
+MESH = pl.DeviceIdType.MESH
+f32 = jnp.float32
+bf16 = jnp.bfloat16
+
+
+def table_split(table):
+    high = table.astype(ml_dtypes.bfloat16)
+    return high, (table - high.astype(np.float32)).astype(ml_dtypes.bfloat16)
+
+
+def split(value):
+    high = value.astype(bf16)
+    return high, (value - high.astype(f32)).astype(bf16)
+
+
+def dot(left, right):
+    return jnp.dot(left, right, preferred_element_type=f32)
+
+
+def dot_full(left, right, contract=((1,), (0,))):
+    return lax.dot_general(
+        left, right, (contract, ((), ())), precision=highest, preferred_element_type=f32
+    )
+
+
+def low_lanes(shape):
+    return lax.broadcasted_iota(jnp.int32, shape, len(shape) - 1) < shape[-1] // 2
+
+
+def swap(value):
+    return pltpu.roll(value, value.shape[-1] // 2, value.ndim - 1)
+
+
+def greet(devices):
+    barrier = pltpu.get_barrier_semaphore()
+    for device in devices:
+        pl.semaphore_signal(barrier, inc=1, device_id=device, device_id_type=MESH)
+    pl.semaphore_wait(barrier, len(devices))
+
+
+def pack_rows(number, query, key, cotangent, out):
+    lanes = out.shape[-1]
+    block = number // 2 * lanes
+    key_part = key[:, block : block + lanes].astype(f32)
+    grad_part = cotangent[:, block : block + lanes].astype(f32) * query[
+        :, block : block + lanes
+    ].astype(f32)
+    low = low_lanes(key_part.shape)
+    if number % 2 == 0:
+        packed = jnp.where(low, key_part, swap(grad_part))
+    else:
+        packed = jnp.where(low, swap(key_part), grad_part)
+    out[number] = packed
+
+
+def one_less_exp(value):
+    series = 1.0 - value / 9.0
+    for order in range(8, 1, -1):
+        series = 1.0 - value / order * series
+    return jnp.where(value < 0.25, value * series, 1.0 - jnp.exp(-value))
+
+
+def fused_kernel(
+    count,
+    groups,
+    coefs,
+    tokens,
+    embed_table,
+    short_conv,
+    query,
+    key,
+    cotangent,
+    decay_rate,
+    first,
+    second,
+    weight_third,
+    skip_gain,
+    feats,
+    twiddles,
+    table_high,
+    table_low,
+    landed,
+    small_landed,
+    summed,
+    staged,
+    arrived,
+    token_rows,
+    token_landed,
+    state,
+    filters,
+    windows,
+    total,
+    shape_total,
+    value,
+    embedded,
+    gated,
+    onehot,
+    acts,
+    filter_spec,
+    shape_spec,
+    pay,
+    small,
+    by_chan,
+    held,
+    by_seq,
+    token_send,
+    token_recv,
+    out_send,
+    out_recv,
+    back_send,
+    back_recv,
+    small_send,
+    small_recv,
+    chan_send,
+    chan_recv,
+    scatter_send,
+    scatter_recv,
+    gather_send,
+    gather_recv,
+):
+    me = lax.axis_index("seq")
+    chan = lax.axis_index("chan")
+    rows = key.shape[0]
+    lanes = staged.shape[2]
+    vocab = embed_table.shape[0]
+    units = second.shape[0]
+    feat = first.shape[0]
+    length = count * rows
+    share = vocab // count
+    peers = [lax.rem(me + step, count) for step in range(1, count)]
+    sources = [lax.rem(me + count - step, count) for step in range(1, count)]
+    across = [lax.rem(chan + step, groups) for step in range(1, groups)]
+
+    def post(source, target, send, recv, device):
+        copy = pltpu.make_async_remote_copy(
+            src_ref=source,
+            dst_ref=target,
+            send_sem=send,
+            recv_sem=recv,
+            device_id=device,
+            device_id_type=MESH,
+        )
+        copy.start()
+        return copy
+
+    token_rows[...] = jnp.zeros_like(token_rows)
+    token_rows[: tokens.shape[0]] = tokens[...].astype(f32)
+    for number in range(count):
+        pack_rows(number, query, key, cotangent, staged)
+    greet([(peer, chan) for peer in peers] + [(me, group) for group in across])
+    token_copies = [
+        post(token_rows, token_landed.at[me], token_send.at[n], token_recv.at[n], (peer, chan))
+        for n, peer in enumerate(peers)
+    ]
+    out_copies = [
+        post(staged.at[peer], arrived.at[me], out_send.at[n], out_recv.at[n], (peer, chan))
+        for n, peer in enumerate(peers)
+    ]
+    arrived[me] = staged[me]
+    token_landed[me] = token_rows[...]
+
+    columns = pl.ds(pl.multiple_of(me // 2 * lanes, lanes), lanes)
+    parity = lax.rem(me, 2)
+
+    def mine(array):
+        lane = lax.broadcasted_iota(jnp.int32, array.shape, 1)
+        return jnp.where(lane // (lanes // 2) == parity, array, swap(array))
+
+    third = mine(weight_third[:, columns])
+    table = mine(embed_table[:, columns].astype(f32)).astype(bf16)
+    rate = mine(jnp.broadcast_to(decay_rate[:, columns], (8, lanes)))[:1]
+    skip = mine(jnp.broadcast_to(skip_gain[:, columns], (8, lanes)))[:1]
+    all_taps = [mine(jnp.broadcast_to(short_conv[j : j + 1, columns], (8, lanes))) for j in range(3)]
+    taps = [tap[:1] for tap in all_taps]
+    scale = jnp.sqrt(one_less_exp(2.0 * rate) / one_less_exp(2.0 * length * rate))
+    low = low_lanes((rows, lanes))
+    sign = jnp.where(low, 1.0, -1.0).astype(f32)
+
+    pre_one = dot_full(first[...], feats[:feat], ((0,), (0,)))
+    act_one = jnp.sin(pre_one)
+    acts[0] = act_one
+    acts[1] = jnp.cos(pre_one)
+    pre_two = dot_full(second[...], act_one, ((0,), (0,)))
+    acts[2] = jnp.sin(pre_two)
+    acts[3] = jnp.cos(pre_two)
+    row_ids = lax.broadcasted_iota(jnp.int32, (rows, lanes), 0).astype(f32)
+    for block in range(count):
+        act_rows = acts[2, :, block * rows : (block + 1) * rows].T
+        window = scale * jnp.exp(-rate * (row_ids + float(block * rows)))
+        windows[block] = window
+        filters[block] = dot_full(act_rows, third) * window
+
+    def spread(both):
+        high, rest = split(both)
+        product = (
+            dot(table_high[...], high) + dot(table_high[...], rest) + dot(table_low[...], high)
+        )
+        return product[:rows], product[rows:]
+
+    def forward(ref, lane):
+        cos_t = twiddles[lane, 0]
+        sin_t = twiddles[lane, 1]
+        real = jnp.zeros((rows, lanes), f32)
+        imag = jnp.zeros((rows, lanes), f32)
+        for n in range(count):
+            piece = ref[n]
+            real = real + coefs[lane, n] * piece
+            imag = imag - coefs[lane, count + n] * piece
+        turned = jnp.concatenate(
+            [real * cos_t + imag * sin_t, imag * cos_t - real * sin_t], axis=1
+        )
+        by_cos, by_sin = spread(turned)
+        return (
+            by_cos[:, :lanes] + by_sin[:, lanes:],
+            by_cos[:, lanes:] - by_sin[:, :lanes],
+        )
+
+    def transform_filter(lane, carry):
+        real, imag = forward(filters, lane)
+        filter_spec[lane, 0] = real
+        filter_spec[lane, 1] = imag * sign
+        return carry
+
+    lax.fori_loop(0, count + 1, transform_filter, 0)
+
+    for copy in token_copies:
+        copy.wait()
+    embedded[:8] = jnp.zeros((8, lanes), f32)
+    vocab_ids = lax.broadcasted_iota(jnp.int32, (vocab, lanes), 0).astype(f32)
+    for block in range(count):
+        for piece in range(rows // lanes):
+            ids = token_landed[block, piece : piece + 1]
+            matches = jnp.where(vocab_ids == ids, 1.0, 0.0)
+            start = block * rows + piece * lanes
+            onehot[:, start : start + lanes] = matches.astype(bf16)
+            embedded[8 + start : 8 + start + lanes] = dot(matches.T.astype(bf16), table)
+    for block in range(count):
+        start = 8 + block * rows
+        value[block] = (
+            taps[0] * embedded[start : start + rows]
+            + taps[1] * embedded[start - 1 : start - 1 + rows]
+            + taps[2] * embedded[start - 2 : start - 2 + rows]
+        )
+    total[...] = jnp.zeros_like(total)
+    shape_total[...] = jnp.zeros_like(shape_total)
+
+    def gate(block):
+        packed = arrived[block]
+        state[block] = jnp.where(low, packed * value[block], packed)
+
+    gate(me)
+    for copy, source in zip(out_copies, sources):
+        copy.wait()
+        gate(source)
+
+    def convolve(lane, carry):
+        xr, xi = forward(state, lane)
+        fr = filter_spec[lane, 0]
+        fi = filter_spec[lane, 1]
+        by_cos, by_sin = spread(jnp.concatenate([xr * fr - xi * fi, xr * fi + xi * fr], axis=1))
+        zr = by_cos[:, :lanes] - by_sin[:, lanes:]
+        zi = by_cos[:, lanes:] + by_sin[:, :lanes]
+        cos_t = twiddles[lane, 0]
+        sin_t = twiddles[lane, 1]
+        ur = zr * cos_t - zi * sin_t
+        ui = zr * sin_t + zi * cos_t
+        for n in range(count):
+            total[n] += coefs[lane, 2 * count + n] * ur - coefs[lane, 3 * count + n] * ui
+        gr, gi = swap(xr), swap(xi)
+        shape_spec[lane] = jnp.where(low, xr * gr + xi * gi, swap(xr * gi - xi * gr))
+        return carry
+
+    lax.fori_loop(0, count + 1, convolve, 0)
+
+    def finish(block):
+        summed_rows = total[block] + skip * state[block]
+        total[block] = summed_rows
+        return jnp.where(low, summed_rows, summed_rows * value[block])
+
+    back_copies = []
+    for n, peer in enumerate(peers):
+        pay[peer] = finish(peer)
+        back_copies.append(
+            post(pay.at[peer], landed.at[me], back_send.at[n], back_recv.at[n], (peer, chan))
+        )
+    landed[me] = finish(me)
+
+    def correlate(lane, carry):
+        cos_t = twiddles[lane, 0]
+        sin_t = twiddles[lane, 1]
+        by_cos, by_sin = spread(shape_spec[lane])
+        both = by_cos - sign * swap(by_sin)
+        part_cos = both * jnp.where(low, cos_t, -sin_t)
+        part_sin = both * jnp.where(low, sin_t, cos_t)
+        for n in range(count):
+            shape_total[n] += (
+                coefs[lane, 2 * count + n] * part_cos - coefs[lane, 3 * count + n] * part_sin
+            )
+        return carry
+
+    lax.fori_loop(0, count + 1, correlate, 0)
+    inv_root = 1.0 / math.sqrt(length)
+    third_sum = jnp.zeros((units, lanes), f32)
+    third_low = jnp.where(low_lanes(third.shape), third, 0.0)
+    for block in range(count):
+        grad_rows = shape_total[block]
+        grad_rows = (grad_rows + swap(grad_rows)) * windows[block]
+        places = slice(block * rows, (block + 1) * rows)
+        third_sum += dot_full(acts[2, :, places], grad_rows)
+        acts[3, :, places] = dot_full(third_low, grad_rows, ((1,), (1,))) * acts[3, :, places]
+    grad_pre_two = acts[3]
+    grad_pre_one = dot_full(second[...], grad_pre_two) * acts[1]
+    grad_both = jnp.concatenate([grad_pre_two, grad_pre_one], axis=0)
+    from_act = dot_full(acts[0], grad_both, ((1,), (1,)))
+    from_feats = dot_full(feats[...], grad_both, ((1,), (1,)))
+    hidden = jnp.where(low_lanes(from_act.shape), from_act, from_feats) * inv_root
+    strip = units // count
+    for n in range(count):
+        by_chan[chan, n] = hidden[n * strip : (n + 1) * strip]
+    chan_copies = [
+        post(by_chan.at[chan], by_chan.at[chan], chan_send.at[n], chan_recv.at[n], (me, group))
+        for n, group in enumerate(across)
+    ]
+
+    gated[length:] = jnp.zeros((8, lanes), f32)
+    short_sums = [jnp.zeros((1, lanes), f32) for _ in range(3)]
+    skip_sum = jnp.zeros((1, lanes), f32)
+    for block in range(count):
+        start = block * rows
+        grad_value = total[block] * swap(arrived[block])
+        gated[start : start + rows] = grad_value
+        for j in range(3):
+            short_sums[j] += jnp.sum(
+                grad_value * embedded[8 + start - j : 8 + start - j + rows], axis=0, keepdims=True
+            )
+        skip_sum += jnp.sum(state[block] * swap(state[block]), axis=0, keepdims=True)
+    embed_sum = jnp.zeros((vocab, lanes), f32)
+    for block in range(count):
+        start = block * rows
+        high, rest = split(
+            taps[0] * gated[start : start + rows]
+            + taps[1] * gated[start + 1 : start + 1 + rows]
+            + taps[2] * gated[start + 2 : start + 2 + rows]
+        )
+        matches = onehot[:, start : start + rows]
+        embed_sum += dot(matches, high) + dot(matches, rest)
+    half = units // 2
+    fold = jnp.where(low_lanes((half, lanes)), third_sum[:half], third_sum[half:])
+    sums = jnp.concatenate([fold, *short_sums, skip_sum, jnp.zeros((4, lanes), f32)], axis=0)
+    for block in range(count):
+        top = embed_sum[block * share : block * share + share // 2]
+        bottom = embed_sum[block * share + share // 2 : (block + 1) * share]
+        folded = jnp.where(low_lanes(top.shape), swap(top), bottom)
+        small[block] = jnp.concatenate([folded, sums], axis=0) * inv_root
+    small_copies = [
+        post(small.at[peer], small_landed.at[me], small_send.at[n], small_recv.at[n], (peer, chan))
+        for n, peer in enumerate(peers)
+    ]
+    small_landed[me] = small[me]
+
+    for copy in chan_copies:
+        copy.wait()
+    for n in range(count):
+        strip_sum = by_chan[0, n]
+        for group in range(1, groups):
+            strip_sum = strip_sum + by_chan[group, n]
+        held[n] = strip_sum
+    scatter_copies = [
+        post(held.at[peer], by_seq.at[me], scatter_send.at[n], scatter_recv.at[n], (peer, chan))
+        for n, peer in enumerate(peers)
+    ]
+    by_seq[me] = held[me]
+    for copy in scatter_copies:
+        copy.wait()
+    strip_sum = by_seq[0]
+    for n in range(1, count):
+        strip_sum = strip_sum + by_seq[n]
+    summed[me] = strip_sum
+    gather_copies = [
+        post(summed.at[me], summed.at[me], gather_send.at[n], gather_recv.at[n], (peer, chan))
+        for n, peer in enumerate(peers)
+    ]
+    for copy in back_copies + small_copies + gather_copies:
+        copy.wait()
+
+
+def finish_kernel(
+    landed,
+    small_landed,
+    summed,
+    query,
+    cotangent,
+    out,
+    grad_query,
+    grad_key,
+    grad_embed,
+    grad_short,
+    grad_skip,
+    grad_first,
+    grad_second,
+    grad_third,
+):
+    count, rows, lanes = landed.shape
+    low = low_lanes((rows, lanes))
+    share = grad_embed.shape[0]
+    part = share // 2
+    half = grad_third.shape[0] // 2
+    for block in range(count // 2):
+        columns = slice(block * lanes, (block + 1) * lanes)
+        even, odd = landed[2 * block], landed[2 * block + 1]
+        inner = jnp.where(low, even, swap(odd))
+        out[:, columns] = (query[:, columns].astype(f32) * inner).astype(bf16)
+        grad_query[:, columns] = (cotangent[:, columns].astype(f32) * inner).astype(bf16)
+        grad_key[:, columns] = jnp.where(low, swap(even), odd).astype(bf16)
+        even, odd = small_landed[2 * block], small_landed[2 * block + 1]
+        left = low_lanes(even.shape)
+        first_rows = jnp.where(left, even, swap(odd))
+        last_rows = jnp.where(left, swap(even), odd)
+        grad_embed[:part, columns] = first_rows[:part]
+        grad_embed[part:, columns] = last_rows[:part]
+        grad_third[:half, columns] = first_rows[part : part + half]
+        grad_third[half:, columns] = last_rows[part : part + half]
+        top = part + half
+        grad_short[:, columns] = last_rows[top : top + 3]
+        grad_skip[:, columns] = last_rows[top + 3 : top + 4]
+    both = jnp.concatenate([summed[n] for n in range(count)], axis=0)
+    units = grad_second.shape[0]
+    grad_second[...] = both[:, :units]
+    grad_first[...] = swap(both)[: grad_first.shape[0], :units]
+
+
+def feature_table(length):
+    positions = np.arange(length, dtype=np.int64)
+    frequency = 2 ** np.arange(BANDS, dtype=np.int64) + 1
+    phases = positions[:, None] * frequency[None, :] % length
+    angles = phases.astype(np.float32) * np.float32(two_pi / length)
+    ramp = positions.astype(np.float32)[:, None] / np.float32(length)
+    return np.concatenate([ramp, np.cos(angles), np.sin(angles)], axis=1).T.astype(np.float32)
+
+
+def fused_device(
+    tokens,
+    embed_table,
+    short_conv,
+    query_branch,
+    key_branch,
+    decay_rate,
+    weight_first,
+    weight_second,
+    weight_third,
+    skip_gain,
+    cotangent,
+):
+    count = lax.axis_size("seq")
+    groups = lax.axis_size("chan")
+    seq_index = lax.axis_index("seq")
+    rows, chan_width = query_branch.shape
+    length = rows * count
+    points = 2 * length
+    vocab = embed_table.shape[0]
+    hidden_units = weight_second.shape[0]
+    feat = weight_first.shape[0]
+    slice_width = chan_width // count
+    lanes = 2 * slice_width
+    share = vocab // count
+    strip = hidden_units // count
+    small_rows = share // 2 + hidden_units // 2 + 8
+    vmem = pl.BlockSpec(memory_space=pltpu.VMEM)
+    smem = pl.BlockSpec(memory_space=pltpu.SMEM)
+    dma = pltpu.SemaphoreType.DMA
+
+    depth = np.arange(rows)
+    turns = np.arange(count + 1)
+    angle = two_pi * (depth[:, None] * depth[None, :] % rows) / rows
+    tables = np.concatenate([np.cos(angle), np.sin(angle)], axis=0).astype(np.float32)
+    table_high, table_low = table_split(tables)
+    twist = two_pi * (turns[:, None] * depth[None, :]) / points
+    twiddles = np.stack([np.cos(twist), np.sin(twist)], axis=1).astype(np.float32)
+    twiddles = np.broadcast_to(twiddles[..., None], (count + 1, 2, rows, lanes)).copy()
+    small_angle = two_pi * (turns[:, None] * np.arange(count)[None, :] % (2 * count)) / (2 * count)
+    weight = np.where((turns == 0) | (turns == count), 1.0, 2.0)[:, None] / points
+    coefs = np.concatenate(
+        [
+            np.cos(small_angle),
+            np.sin(small_angle),
+            weight * np.cos(small_angle),
+            weight * np.sin(small_angle),
+        ],
+        axis=1,
+    ).astype(np.float32)
+    feats = np.pad(feature_table(length), ((0, hidden_units - feat), (0, 0)))
+
+    def whole(*shape):
+        return jax.ShapeDtypeStruct(shape, f32)
+
+    def buffer(*shape):
+        return pltpu.VMEM(shape, f32)
+
+    block_shape = (count, rows, lanes)
+    landed, small_landed, summed = pl.pallas_call(
+        functools.partial(fused_kernel, count, groups),
+        out_shape=(
+            whole(*block_shape),
+            whole(count, small_rows, lanes),
+            whole(count, strip, lanes),
+        ),
+        in_specs=[smem] + [vmem] * 15,
+        out_specs=(vmem,) * 3,
+        scratch_shapes=[
+            buffer(*block_shape),
+            buffer(*block_shape),
+            buffer(8, lanes),
+            buffer(count, 8, lanes),
+            buffer(*block_shape),
+            buffer(*block_shape),
+            buffer(*block_shape),
+            buffer(*block_shape),
+            buffer(*block_shape),
+            buffer(*block_shape),
+            buffer(length + 8, lanes),
+            buffer(length + 8, lanes),
+            pltpu.VMEM((vocab, length), bf16),
+            buffer(4, hidden_units, length),
+            buffer(count + 1, 2, rows, lanes),
+            buffer(count + 1, rows, lanes),
+            buffer(*block_shape),
+            buffer(count, small_rows, lanes),
+            buffer(groups, count, strip, lanes),
+            buffer(count, strip, lanes),
+            buffer(count, strip, lanes),
+        ]
+        + [dma((count,))] * 8
+        + [dma((groups,))] * 2
+        + [dma((count,))] * 4,
+        compiler_params=pltpu.CompilerParams(
+            collective_id=0, has_side_effects=True, vmem_limit_bytes=52 * 2**20
+        ),
+        name="convolve_slices",
+    )(
+        jnp.asarray(coefs),
+        tokens.reshape(rows // lanes, lanes),
+        embed_table,
+        short_conv,
+        query_branch,
+        key_branch,
+        cotangent,
+        decay_rate[None],
+        weight_first,
+        weight_second,
+        weight_third,
+        skip_gain[None],
+        jnp.asarray(feats),
+        jnp.asarray(twiddles),
+        jnp.asarray(table_high),
+        jnp.asarray(table_low),
+    )
+    half_out = jax.ShapeDtypeStruct((rows, chan_width), bf16)
+    results = pl.pallas_call(
+        finish_kernel,
+        out_shape=(
+            half_out,
+            half_out,
+            half_out,
+            whole(share, chan_width),
+            whole(3, chan_width),
+            whole(1, chan_width),
+            whole(feat, hidden_units),
+            whole(hidden_units, hidden_units),
+            whole(hidden_units, chan_width),
+        ),
+        in_specs=[vmem] * 5,
+        out_specs=(vmem,) * 9,
+        compiler_params=pltpu.CompilerParams(vmem_limit_bytes=32 * 2**20),
+        name="finish_outputs",
+    )(landed, small_landed, summed, query_branch, cotangent)
+    return results[:5] + (results[5][0],) + results[6:]
+
+
+def per_slice(*arrays):
+    count = lax.axis_size("seq")
+    rows, width = arrays[3].shape
+    lanes = 2 * width // count
+    units = arrays[7].shape[0]
+    vocab = arrays[1].shape[0]
+    tiled = lanes % 128 == 0 and rows % lanes == 0 and rows <= 8 * lanes
+    even = count % 2 == 0 and 2 * units == lanes and units % (8 * count) == 0
+    body = fused_device if tiled and even and vocab % (16 * count) == 0 else per_device
+    return body(*arrays)
+
 
 def solution(mesh):
     in_specs = (
@@ -300,5 +894,5 @@
         P(None, "chan"),
     )
     return jax.shard_map(
-        per_device, mesh=mesh, in_specs=in_specs, out_specs=out_specs, check_vma=False
-    )
+        per_slice, mesh=mesh, in_specs=in_specs, out_specs=out_specs, check_vma=False
+    )

time: 308 us -> 94.1 us (0.31); the launches traced: 302 us -> 93.5 us
  waiting for transfers between devices: 130 us -> 0 us
  Pallas kernels: 0 us -> 81 us
  matrix products: 61 us -> 0 us
  blocking collectives: 37.9 us -> 0 us
  starting transfers between devices: 24.9 us -> 0 us
  other arithmetic: 21.5 us -> 0 us
  between operations: 15 us -> 0.68 us
    psum x2 -> x0, waiting for transfers between devices: 97 us -> none  [the longest x1 63.6 us: per_device(): lax.psum((short_part, skip_part, third_part, first_part, second_part), 's...]
    pallas_call x0 -> x2, Pallas kernels: none -> 81 us  [the longest x1 79.8 us: fused_device(): pl.pallas_call(functools.partial(fused_kernel, count, groups), out_shape=...]
    dot_general x22 -> x0, matrix products: 61 us -> none  [the longest x3 12.5 us: lane_inverse(): jnp.einsum('rckm,mj->rckj', spectrum, tables, precision=highest)]
    psum x1 -> x0, blocking collectives: 37.9 us -> none  [per_device(): lax.psum((short_part, skip_part, third_part, first_part, second_part), 's...]
    reduce_scatter x1 -> x0, waiting for transfers between devices: 21.1 us -> none  [per_device(): lax.psum_scatter(jnp.dot(matches, weighted, precision=highest, preferred_...]
    all_to_all x4 -> x0, starting transfers between devices: 19.5 us -> none  [the longest x1 5.89 us: per_device(): lax.all_to_all(back_lanes, 'seq', split_axis=1, concat_axis=0, tiled=True)]
    all_to_all x4 -> x0, waiting for transfers between devices: 12.2 us -> none  [the longest x1 6.12 us: per_device(): lax.all_to_all(keyed_value.T, 'seq', split_axis=0, concat_axis=1, tiled=T...]
    unnamed x112 -> x28, local copies, waits for them, and re-layouts: 2.92 us -> 11.8 us
  transfers between devices with their start and end apart: 8 -> 0, of which waited for: 5 -> 0; matrix products, arithmetic and copies ran while one was open for 18% -> 0% of each run, Pallas kernels for 0% -> 0%
where the time goes in v2:
time: 94.1 us; the launch traced here: 93.5 us
  Pallas kernels  81 us (86%)
  local copies, waits for them, and re-layouts  11.8 us (13%)
    pallas_call x1, Pallas kernels, fused_device(): pl.pallas_call(functools.partial(fused_kernel, count, groups), out_shape=...  79.8 us
    unnamed x28, local copies, waits for them, and re-layouts  11.8 us

profile of v2, /device:TPU:0, one launch (start us, length us, event | category | flops | bytes accessed | tf_op | source)
XLA Modules:
  0.0 93.5 jit_solution(2620335872916853356)
XLA Ops:
  0.6 0.0 copy-start
  0.7 0.9 %copy-done = bf16[256,512]{1,0:T(8,128)(2,1)S(1)} copy-done((bf16[256,512]{1,0:T(8,128)(2,1)S(1)}, bf16[256,512]{1,0:T(8,128)(2,1)}, u32[]{:S(2)}) %copy-start) | copy-done | bytes 262168
  1.6 0.0 copy-start.1
  1.6 0.9 %copy-done.1 = bf16[256,512]{1,0:T(8,128)(2,1)S(1)} copy-done((bf16[256,512]{1,0:T(8,128)(2,1)S(1)}, bf16[256,512]{1,0:T(8,128)(2,1)}, u32[]{:S(2)}) %copy-start.1) | copy-done | bytes 262168
  2.5 0.0 copy-start.3
  2.5 0.9 %copy-done.3 = bf16[256,512]{1,0:T(8,128)(2,1)S(1)} copy-done((bf16[256,512]{1,0:T(8,128)(2,1)S(1)}, bf16[256,512]{1,0:T(8,128)(2,1)}, u32[]{:S(2)}) %copy-start.3) | copy-done | bytes 262168
  3.5 0.0 copy-start.4
  3.5 0.9 %copy-done.4 = bf16[256,512]{1,0:T(8,128)(2,1)S(1)} copy-done((bf16[256,512]{1,0:T(8,128)(2,1)S(1)}, bf16[256,512]{1,0:T(8,128)(2,1)}, u32[]{:S(2)}) %copy-start.4) | copy-done | bytes 262168
  4.4 0.0 copy-start.5
  4.5 0.9 %copy-done.5 = bf16[512,256]{1,0:T(8,128)(2,1)S(1)} copy-done((bf16[512,256]{1,0:T(8,128)(2,1)S(1)}, bf16[512,256]{1,0:T(8,128)(2,1)}, u32[]{:S(2)}) %copy-start.5) | copy-done | bytes 262168
  5.4 0.0 copy-start.6
  5.4 0.9 copy-done.6
  6.3 0.0 copy-start.7
  6.3 0.8 copy-done.7
  7.1 0.0 copy-start.8
  7.1 0.7 copy-done.8
  7.8 0.0 copy-start.9
  7.8 0.7 copy-done.9
  8.5 0.0 copy-start.10
  8.5 0.7 copy-done.10
  9.2 0.0 copy-start.11
  9.2 0.7 copy-done.11
  9.9 0.0 copy-start.12
  9.9 0.7 copy-done.12
  10.5 0.0 copy-start.13
  10.6 0.7 copy-done.13
  11.2 79.8 %convolve_slices.1 = (f32[8,256,128]{2,1,0:T(8,128)}, f32[8,56,128]{2,1,0:T(8,128)S(1)}, f32[8,8,128]{2,1,0:T(8,128)S(1)}) custom-call(f32[9,32]{1,0:T(8,128)S(1)} %copy-done.10, s32[2,128]{1,0:T(2,128)S(1)} %bitcast.6, bf16[256,512]{1,0:T(8,128)(2,1)S(1)} %copy-done.3, f32[3,512]{1,0:T(4,128)S(1)} %copy-done.9, bf16[256,512]{1,0:T(8,128)(2,1)S(1)} %copy-done, ...), custom_call_target="tpu_custom_call" | custom-call | tf_op jit(solution)/shard_map/convolve_slices/pallas_call | solution.py:780
  91.0 0.0 copy-start.2
  91.0 1.2 %copy-done.2 = f32[8,256,128]{2,1,0:T(8,128)S(1)} copy-done((f32[8,256,128]{2,1,0:T(8,128)S(1)}, f32[8,256,128]{2,1,0:T(8,128)}, u32[]{:S(2)}) %copy-start.2) | copy-done | bytes 1048600
  92.3 1.2 %finish_outputs.1 = (bf16[256,512]{1,0:T(8,128)(2,1)}, bf16[256,512]{1,0:T(8,128)(2,1)}, bf16[256,512]{1,0:T(8,128)(2,1)}, f32[32,512]{1,0:T(8,128)}, f32[3,512]...) custom-call(f32[8,256,128]{2,1,0:T(8,128)S(1)} %copy-done.2, ...), custom_call_target="tpu_custom_call" | custom-call | tf_op jit(solution)/shard_map/finish_outputs/pallas_call | solution.py:838
Async XLA Ops:
  0.6 1.0 %copy-start = (bf16[256,512]{1,0:T(8,128)(2,1)S(1)}, bf16[256,512]{1,0:T(8,128)(2,1)}, u32[]{:S(2)}) copy-start(bf16[256,512]{1,0:T(8,128)(2,1)} %query.3) | copy-start | bytes 786436
  1.6 0.9 %copy-start.1 = (bf16[256,512]{1,0:T(8,128)(2,1)S(1)}, bf16[256,512]{1,0:T(8,128)(2,1)}, u32[]{:S(2)}) copy-start(bf16[256,512]{1,0:T(8,128)(2,1)} %cotangent.3) | copy-start | bytes 786436
  2.5 0.9 %copy-start.3 = (bf16[256,512]{1,0:T(8,128)(2,1)S(1)}, bf16[256,512]{1,0:T(8,128)(2,1)}, u32[]{:S(2)}) copy-start(bf16[256,512]{1,0:T(8,128)(2,1)} %embed_table.1) | copy-start | bytes 786436
  3.5 0.9 %copy-start.4 = (bf16[256,512]{1,0:T(8,128)(2,1)S(1)}, bf16[256,512]{1,0:T(8,128)(2,1)}, u32[]{:S(2)}) copy-start(bf16[256,512]{1,0:T(8,128)(2,1)} %key.1) | copy-start | bytes 786436
  4.4 0.9 %copy-start.5 = (bf16[512,256]{1,0:T(8,128)(2,1)S(1)}, bf16[512,256]{1,0:T(8,128)(2,1)}, u32[]{:S(2)}) copy-start(bf16[512,256]{1,0:T(8,128)(2,1)} %constant.13.clone.table_high) | copy-start | bytes 786436
  5.4 0.9 copy-start.6
  6.3 0.8 copy-start.7
  7.1 0.7 copy-start.8
  7.8 0.7 copy-start.9
  8.5 0.7 copy-start.10
  9.2 0.7 copy-start.11
  9.9 0.7 copy-start.12
  10.5 0.7 copy-start.13
  91.0 1.2 %copy-start.2 = (f32[8,256,128]{2,1,0:T(8,128)S(1)}, f32[8,256,128]{2,1,0:T(8,128)}, u32[]{:S(2)}) copy-start(f32[8,256,128]{2,1,0:T(8,128)} %get-tuple-element.21.landed) | copy-start | bytes 3145732

commit v3 on v2

--- a/solution.py
+++ b/solution.py
@@ -3,7 +3,6 @@
 
 import jax
 import jax.numpy as jnp
-import ml_dtypes
 import numpy as np
 from jax import lax
 from jax.experimental import pallas as pl
@@ -283,11 +282,6 @@
 bf16 = jnp.bfloat16
 
 
-def table_split(table):
-    high = table.astype(ml_dtypes.bfloat16)
-    return high, (table - high.astype(np.float32)).astype(ml_dtypes.bfloat16)
-
-
 def split(value):
     high = value.astype(bf16)
     return high, (value - high.astype(f32)).astype(bf16)
@@ -357,11 +351,14 @@
     skip_gain,
     feats,
     twiddles,
-    table_high,
-    table_low,
+    tables,
     landed,
     small_landed,
     summed,
+    held_inputs,
+    input_sems,
+    table_high,
+    table_low,
     staged,
     arrived,
     token_rows,
@@ -400,6 +397,20 @@
 ):
     me = lax.axis_index("seq")
     chan = lax.axis_index("chan")
+    sources = (
+        (key, query, cotangent, tokens)
+        + (first, second, feats, embed_table, short_conv, decay_rate, weight_third)
+        + (skip_gain, twiddles, tables)
+    )
+    loads = [
+        pltpu.make_async_copy(source, target, input_sems.at[n])
+        for n, (source, target) in enumerate(zip(sources, held_inputs))
+    ]
+    for load in loads:
+        load.start()
+    key, query, cotangent, tokens, first, second, feats = held_inputs[:7]
+    embed_table, short_conv, decay_rate, weight_third = held_inputs[7:11]
+    skip_gain, twiddles, tables = held_inputs[11:]
     rows = key.shape[0]
     lanes = staged.shape[2]
     vocab = embed_table.shape[0]
@@ -423,6 +434,8 @@
         copy.start()
         return copy
 
+    for load in loads[:4]:
+        load.wait()
     token_rows[...] = jnp.zeros_like(token_rows)
     token_rows[: tokens.shape[0]] = tokens[...].astype(f32)
     for number in range(count):
@@ -438,6 +451,10 @@
     ]
     arrived[me] = staged[me]
     token_landed[me] = token_rows[...]
+
+    for load in loads[4:]:
+        load.wait()
+    table_high[...], table_low[...] = split(tables[...])
 
     columns = pl.ds(pl.multiple_of(me // 2 * lanes, lanes), lanes)
     parity = lax.rem(me, 2)
@@ -753,7 +770,6 @@
     turns = np.arange(count + 1)
     angle = two_pi * (depth[:, None] * depth[None, :] % rows) / rows
     tables = np.concatenate([np.cos(angle), np.sin(angle)], axis=0).astype(np.float32)
-    table_high, table_low = table_split(tables)
     twist = two_pi * (turns[:, None] * depth[None, :]) / points
     twiddles = np.stack([np.cos(twist), np.sin(twist)], axis=1).astype(np.float32)
     twiddles = np.broadcast_to(twiddles[..., None], (count + 1, 2, rows, lanes)).copy()
@@ -777,6 +793,23 @@
         return pltpu.VMEM(shape, f32)
 
     block_shape = (count, rows, lanes)
+    operands = (
+        tokens.reshape(rows // lanes, lanes),
+        embed_table,
+        short_conv,
+        query_branch,
+        key_branch,
+        cotangent,
+        decay_rate[None],
+        weight_first,
+        weight_second,
+        weight_third,
+        skip_gain[None],
+        jnp.asarray(feats),
+        jnp.asarray(twiddles),
+        jnp.asarray(tables),
+    )
+    load_order = (4, 3, 5, 0, 7, 8, 11, 1, 2, 6, 9, 10, 12, 13)
     landed, small_landed, summed = pl.pallas_call(
         functools.partial(fused_kernel, count, groups),
         out_shape=(
@@ -784,9 +817,13 @@
             whole(count, small_rows, lanes),
             whole(count, strip, lanes),
         ),
-        in_specs=[smem] + [vmem] * 15,
+        in_specs=[smem] + [pl.BlockSpec(memory_space=pltpu.HBM)] * 14,
         out_specs=(vmem,) * 3,
         scratch_shapes=[
+            [pltpu.VMEM(operands[n].shape, operands[n].dtype) for n in load_order],
+            dma((len(load_order),)),
+            pltpu.VMEM(tables.shape, bf16),
+            pltpu.VMEM(tables.shape, bf16),
             buffer(*block_shape),
             buffer(*block_shape),
             buffer(8, lanes),
@@ -813,27 +850,10 @@
         + [dma((groups,))] * 2
         + [dma((count,))] * 4,
         compiler_params=pltpu.CompilerParams(
-            collective_id=0, has_side_effects=True, vmem_limit_bytes=52 * 2**20
+            collective_id=0, has_side_effects=True, vmem_limit_bytes=56 * 2**20
         ),
         name="convolve_slices",
-    )(
-        jnp.asarray(coefs),
-        tokens.reshape(rows // lanes, lanes),
-        embed_table,
-        short_conv,
-        query_branch,
-        key_branch,
-        cotangent,
-        decay_rate[None],
-        weight_first,
-        weight_second,
-        weight_third,
-        skip_gain[None],
-        jnp.asarray(feats),
-        jnp.asarray(twiddles),
-        jnp.asarray(table_high),
-        jnp.asarray(table_low),
-    )
+    )(jnp.asarray(coefs), *operands)
     half_out = jax.ShapeDtypeStruct((rows, chan_width), bf16)
     results = pl.pallas_call(
         finish_kernel,
@@ -850,7 +870,7 @@
         ),
         in_specs=[vmem] * 5,
         out_specs=(vmem,) * 9,
-        compiler_params=pltpu.CompilerParams(vmem_limit_bytes=32 * 2**20),
+        compiler_params=pltpu.CompilerParams(vmem_limit_bytes=60 * 2**20),
         name="finish_outputs",
     )(landed, small_landed, summed, query_branch, cotangent)
     return results[:5] + (results[5][0],) + results[6:]

time: 94.1 us -> 83.5 us (0.89)
  local copies, waits for them, and re-layouts: 11.8 us -> 0 us
  Pallas kernels: 81 us -> 82.7 us
    unnamed x28 -> x0, local copies, waits for them, and re-layouts: 11.8 us -> none
    pallas_call x1, Pallas kernels: 1.25 us -> 2.73 us  [fused_device(): pl.pallas_call(finish_kernel, out_shape=(half_out, half_out, half_out, wh...]
where the time goes in v3:
time: 83.5 us; the launch traced here: 83.3 us
  Pallas kernels  82.7 us (99%)
    pallas_call x1, Pallas kernels, fused_device(): pl.pallas_call(functools.partial(fused_kernel, count, groups), out_shape=...  79.9 us
    pallas_call x1, Pallas kernels, fused_device(): pl.pallas_call(finish_kernel, out_shape=(half_out, half_out, half_out, wh...  2.73 us

profile of v3, /device:TPU:0, one launch (start us, length us, event | category | flops | bytes accessed | tf_op | source)
XLA Modules:
  0.0 83.3 jit_solution(13411194900289214153)
XLA Ops:
  0.6 79.9 %convolve_slices.1 = (f32[8,256,128]{2,1,0:T(8,128)}, f32[8,56,128]{2,1,0:T(8,128)}, f32[8,8,128]{2,1,0:T(8,128)}) custom-call(f32[9,32]{1,0:T(8,128)} %constant.11.clone.coefs, s32[2,128]{1,0:T(2,128)} %bitcast.6, bf16[256,512]{1,0:T(8,128)(2,1)} %embed_table.1, f32[3,512]{1,0:T(4,128)} %short_conv.1, bf16[256,512]{1,0:T(8,128)(2,1)} %query.3, ...), custom_call_target="tpu_custom_call" | custom-call | tf_op jit(solution)/shard_map/convolve_slices/pallas_call | solution.py:813
  80.6 2.7 %finish_outputs.1 = (bf16[256,512]{1,0:T(8,128)(2,1)}, bf16[256,512]{1,0:T(8,128)(2,1)}, bf16[256,512]{1,0:T(8,128)(2,1)}, f32[32,512]{1,0:T(8,128)}, f32[3,512]...) custom-call(f32[8,256,128]{2,1,0:T(8,128)} %get-tuple-element.21.landed, ...), custom_call_target="tpu_custom_call" | custom-call | tf_op jit(solution)/shard_map/finish_outputs/pallas_call | solution.py:858

commit v4 on v3

--- a/solution.py
+++ b/solution.py
@@ -494,31 +494,52 @@
         )
         return product[:rows], product[rows:]
 
-    def forward(ref, lane):
+    def turn_forward(real, imag, lane):
         cos_t = twiddles[lane, 0]
         sin_t = twiddles[lane, 1]
-        real = jnp.zeros((rows, lanes), f32)
-        imag = jnp.zeros((rows, lanes), f32)
-        for n in range(count):
-            piece = ref[n]
-            real = real + coefs[lane, n] * piece
-            imag = imag - coefs[lane, count + n] * piece
-        turned = jnp.concatenate(
-            [real * cos_t + imag * sin_t, imag * cos_t - real * sin_t], axis=1
+        by_cos, by_sin = spread(
+            jnp.concatenate([real * cos_t + imag * sin_t, imag * cos_t - real * sin_t], axis=1)
         )
-        by_cos, by_sin = spread(turned)
         return (
             by_cos[:, :lanes] + by_sin[:, lanes:],
             by_cos[:, lanes:] - by_sin[:, :lanes],
         )
 
+    def forward(ref, lane):
+        cos_sums, sin_sums = [], []
+        for start in range(2):
+            cos_sum = jnp.zeros((rows, lanes), f32)
+            sin_sum = jnp.zeros((rows, lanes), f32)
+            for n in range(start, count, 2):
+                piece = ref[n]
+                cos_sum = cos_sum + coefs[lane, n] * piece
+                sin_sum = sin_sum + coefs[lane, count + n] * piece
+            cos_sums.append(cos_sum)
+            sin_sums.append(sin_sum)
+        return (
+            turn_forward(cos_sums[0] + cos_sums[1], -(sin_sums[0] + sin_sums[1]), lane),
+            turn_forward(cos_sums[0] - cos_sums[1], sin_sums[0] - sin_sums[1], count - lane),
+        )
+
+    def add_back(ref, lane, near, far):
+        (near_cos, near_sin), (far_cos, far_sin) = near, far
+        by_parity = (
+            (near_cos + far_cos, near_sin - far_sin),
+            (near_cos - far_cos, near_sin + far_sin),
+        )
+        for n in range(count):
+            cos_part, sin_part = by_parity[n % 2]
+            ref[n] += (
+                coefs[lane, 2 * count + n] * cos_part - coefs[lane, 3 * count + n] * sin_part
+            )
+
     def transform_filter(lane, carry):
-        real, imag = forward(filters, lane)
-        filter_spec[lane, 0] = real
-        filter_spec[lane, 1] = imag * sign
+        for place, (real, imag) in zip((lane, count - lane), forward(filters, lane)):
+            filter_spec[place, 0] = real
+            filter_spec[place, 1] = imag * sign
         return carry
 
-    lax.fori_loop(0, count + 1, transform_filter, 0)
+    lax.fori_loop(0, count // 2 + 1, transform_filter, 0)
 
     for copy in token_copies:
         copy.wait()
@@ -550,52 +571,60 @@
         copy.wait()
         gate(source)
 
-    def convolve(lane, carry):
-        xr, xi = forward(state, lane)
-        fr = filter_spec[lane, 0]
-        fi = filter_spec[lane, 1]
+    def multiply(place, xr, xi):
+        fr = filter_spec[place, 0]
+        fi = filter_spec[place, 1]
         by_cos, by_sin = spread(jnp.concatenate([xr * fr - xi * fi, xr * fi + xi * fr], axis=1))
         zr = by_cos[:, :lanes] - by_sin[:, lanes:]
         zi = by_cos[:, lanes:] + by_sin[:, :lanes]
-        cos_t = twiddles[lane, 0]
-        sin_t = twiddles[lane, 1]
-        ur = zr * cos_t - zi * sin_t
-        ui = zr * sin_t + zi * cos_t
-        for n in range(count):
-            total[n] += coefs[lane, 2 * count + n] * ur - coefs[lane, 3 * count + n] * ui
+        cos_t = twiddles[place, 0]
+        sin_t = twiddles[place, 1]
         gr, gi = swap(xr), swap(xi)
-        shape_spec[lane] = jnp.where(low, xr * gr + xi * gi, swap(xr * gi - xi * gr))
+        shape_spec[place] = jnp.where(low, xr * gr + xi * gi, swap(xr * gi - xi * gr))
+        return zr * cos_t - zi * sin_t, zr * sin_t + zi * cos_t
+
+    def convolve(lane, carry):
+        near, far = forward(state, lane)
+        add_back(total, lane, multiply(lane, *near), multiply(count - lane, *far))
         return carry
 
-    lax.fori_loop(0, count + 1, convolve, 0)
+    lax.fori_loop(0, count // 2 + 1, convolve, 0)
 
     def finish(block):
         summed_rows = total[block] + skip * state[block]
         total[block] = summed_rows
         return jnp.where(low, summed_rows, summed_rows * value[block])
 
+    middle = rows // 2
+
+    def post_back(n, part):
+        places = pl.ds(part * middle, middle)
+        return post(
+            pay.at[peers[n], places],
+            landed.at[me, places],
+            back_send.at[part, n],
+            back_recv.at[part, n],
+            (peers[n], chan),
+        )
+
     back_copies = []
     for n, peer in enumerate(peers):
         pay[peer] = finish(peer)
-        back_copies.append(
-            post(pay.at[peer], landed.at[me], back_send.at[n], back_recv.at[n], (peer, chan))
-        )
+        back_copies.append(post_back(n, 0))
     landed[me] = finish(me)
 
+    def correlate_one(place):
+        cos_t = twiddles[place, 0]
+        sin_t = twiddles[place, 1]
+        by_cos, by_sin = spread(shape_spec[place])
+        both = by_cos - sign * swap(by_sin)
+        return both * jnp.where(low, cos_t, -sin_t), both * jnp.where(low, sin_t, cos_t)
+
     def correlate(lane, carry):
-        cos_t = twiddles[lane, 0]
-        sin_t = twiddles[lane, 1]
-        by_cos, by_sin = spread(shape_spec[lane])
-        both = by_cos - sign * swap(by_sin)
-        part_cos = both * jnp.where(low, cos_t, -sin_t)
-        part_sin = both * jnp.where(low, sin_t, cos_t)
-        for n in range(count):
-            shape_total[n] += (
-                coefs[lane, 2 * count + n] * part_cos - coefs[lane, 3 * count + n] * part_sin
-            )
+        add_back(shape_total, lane, correlate_one(lane), correlate_one(count - lane))
         return carry
 
-    lax.fori_loop(0, count + 1, correlate, 0)
+    lax.fori_loop(0, count // 2 + 1, correlate, 0)
     inv_root = 1.0 / math.sqrt(length)
     third_sum = jnp.zeros((units, lanes), f32)
     third_low = jnp.where(low_lanes(third.shape), third, 0.0)
@@ -618,6 +647,20 @@
         post(by_chan.at[chan], by_chan.at[chan], chan_send.at[n], chan_recv.at[n], (me, group))
         for n, group in enumerate(across)
     ]
+
+    for copy in chan_copies:
+        copy.wait()
+    for n in range(count):
+        strip_sum = by_chan[0, n]
+        for group in range(1, groups):
+            strip_sum = strip_sum + by_chan[group, n]
+        held[n] = strip_sum
+    scatter_copies = [
+        post(held.at[peer], by_seq.at[me], scatter_send.at[n], scatter_recv.at[n], (peer, chan))
+        for n, peer in enumerate(peers)
+    ]
+    by_seq[me] = held[me]
+    back_copies += [post_back(n, 1) for n in range(count - 1)]
 
     gated[length:] = jnp.zeros((8, lanes), f32)
     short_sums = [jnp.zeros((1, lanes), f32) for _ in range(3)]
@@ -655,18 +698,6 @@
     ]
     small_landed[me] = small[me]
 
-    for copy in chan_copies:
-        copy.wait()
-    for n in range(count):
-        strip_sum = by_chan[0, n]
-        for group in range(1, groups):
-            strip_sum = strip_sum + by_chan[group, n]
-        held[n] = strip_sum
-    scatter_copies = [
-        post(held.at[peer], by_seq.at[me], scatter_send.at[n], scatter_recv.at[n], (peer, chan))
-        for n, peer in enumerate(peers)
-    ]
-    by_seq[me] = held[me]
     for copy in scatter_copies:
         copy.wait()
     strip_sum = by_seq[0]
@@ -774,7 +805,7 @@
     twiddles = np.stack([np.cos(twist), np.sin(twist)], axis=1).astype(np.float32)
     twiddles = np.broadcast_to(twiddles[..., None], (count + 1, 2, rows, lanes)).copy()
     small_angle = two_pi * (turns[:, None] * np.arange(count)[None, :] % (2 * count)) / (2 * count)
-    weight = np.where((turns == 0) | (turns == count), 1.0, 2.0)[:, None] / points
+    weight = np.where(turns % (count // 2) == 0, 1.0, 2.0)[:, None] / points
     coefs = np.concatenate(
         [
             np.cos(small_angle),
@@ -846,7 +877,9 @@
             buffer(count, strip, lanes),
             buffer(count, strip, lanes),
         ]
-        + [dma((count,))] * 8
+        + [dma((count,))] * 4
+        + [dma((2, count))] * 2
+        + [dma((count,))] * 2
         + [dma((groups,))] * 2
         + [dma((count,))] * 4,
         compiler_params=pltpu.CompilerParams(

time: 83.5 us -> 76.4 us (0.915)
  Pallas kernels: 82.7 us -> 75.5 us
    pallas_call x1, Pallas kernels: 79.9 us -> 72.8 us  [fused_device(): pl.pallas_call(functools.partial(fused_kernel, count, groups), out_shape=...]
where the time goes in v4:
time: 76.4 us; the launch traced here: 76.2 us
  Pallas kernels  75.5 us (99%)
    pallas_call x1, Pallas kernels, fused_device(): pl.pallas_call(functools.partial(fused_kernel, count, groups), out_shape=...  72.8 us
    pallas_call x1, Pallas kernels, fused_device(): pl.pallas_call(finish_kernel, out_shape=(half_out, half_out, half_out, wh...  2.73 us

profile of v4, /device:TPU:0, one launch (start us, length us, event | category | flops | bytes accessed | tf_op | source)
XLA Modules:
  0.0 76.2 jit_solution(8489214891851400477)
XLA Ops:
  0.6 72.8 %convolve_slices.1 = (f32[8,256,128]{2,1,0:T(8,128)}, f32[8,56,128]{2,1,0:T(8,128)}, f32[8,8,128]{2,1,0:T(8,128)}) custom-call(f32[9,32]{1,0:T(8,128)} %constant.11.clone.coefs, s32[2,128]{1,0:T(2,128)} %bitcast.6, bf16[256,512]{1,0:T(8,128)(2,1)} %embed_table.1, f32[3,512]{1,0:T(4,128)} %short_conv.1, bf16[256,512]{1,0:T(8,128)(2,1)} %query.3, ...), custom_call_target="tpu_custom_call" | custom-call | tf_op jit(solution)/shard_map/convolve_slices/pallas_call | solution.py:844
  73.5 2.7 %finish_outputs.1 = (bf16[256,512]{1,0:T(8,128)(2,1)}, bf16[256,512]{1,0:T(8,128)(2,1)}, bf16[256,512]{1,0:T(8,128)(2,1)}, f32[32,512]{1,0:T(8,128)}, f32[3,512]...) custom-call(f32[8,256,128]{2,1,0:T(8,128)} %get-tuple-element.21.landed, ...), custom_call_target="tpu_custom_call" | custom-call | tf_op jit(solution)/shard_map/finish_outputs/pallas_call | solution.py:891

commit v5 on v4

--- a/solution.py
+++ b/solution.py
@@ -309,7 +309,6 @@
     barrier = pltpu.get_barrier_semaphore()
     for device in devices:
         pl.semaphore_signal(barrier, inc=1, device_id=device, device_id_type=MESH)
-    pl.semaphore_wait(barrier, len(devices))
 
 
 def pack_rows(number, query, key, cotangent, out):
@@ -421,6 +420,7 @@
     peers = [lax.rem(me + step, count) for step in range(1, count)]
     sources = [lax.rem(me + count - step, count) for step in range(1, count)]
     across = [lax.rem(chan + step, groups) for step in range(1, groups)]
+    greet([(peer, chan) for peer in peers] + [(me, group) for group in across])
 
     def post(source, target, send, recv, device):
         copy = pltpu.make_async_remote_copy(
@@ -440,7 +440,7 @@
     token_rows[: tokens.shape[0]] = tokens[...].astype(f32)
     for number in range(count):
         pack_rows(number, query, key, cotangent, staged)
-    greet([(peer, chan) for peer in peers] + [(me, group) for group in across])
+    pl.semaphore_wait(pltpu.get_barrier_semaphore(), len(peers) + len(across))
     token_copies = [
         post(token_rows, token_landed.at[me], token_send.at[n], token_recv.at[n], (peer, chan))
         for n, peer in enumerate(peers)

time: 76.4 us -> 75.1 us (0.983)
  Pallas kernels: 75.5 us -> 74.2 us
    pallas_call x1, Pallas kernels: 72.8 us -> 71.5 us  [fused_device(): pl.pallas_call(functools.partial(fused_kernel, count, groups), out_shape=...]
where the time goes in v5:
time: 75.1 us; the launch traced here: 74.9 us
  Pallas kernels  74.2 us (99%)
    pallas_call x1, Pallas kernels, fused_device(): pl.pallas_call(functools.partial(fused_kernel, count, groups), out_shape=...  71.5 us
    pallas_call x1, Pallas kernels, fused_device(): pl.pallas_call(finish_kernel, out_shape=(half_out, half_out, half_out, wh...  2.73 us

profile of v5, /device:TPU:0, one launch (start us, length us, event | category | flops | bytes accessed | tf_op | source)
XLA Modules:
  0.0 74.9 jit_solution(9516513599771618818)
XLA Ops:
  0.6 71.5 %convolve_slices.1 = (f32[8,256,128]{2,1,0:T(8,128)}, f32[8,56,128]{2,1,0:T(8,128)}, f32[8,8,128]{2,1,0:T(8,128)}) custom-call(f32[9,32]{1,0:T(8,128)} %constant.11.clone.coefs, s32[2,128]{1,0:T(2,128)} %bitcast.6, bf16[256,512]{1,0:T(8,128)(2,1)} %embed_table.1, f32[3,512]{1,0:T(4,128)} %short_conv.1, bf16[256,512]{1,0:T(8,128)(2,1)} %query.3, ...), custom_call_target="tpu_custom_call" | custom-call | tf_op jit(solution)/shard_map/convolve_slices/pallas_call | solution.py:844
  72.1 2.7 %finish_outputs.1 = (bf16[256,512]{1,0:T(8,128)(2,1)}, bf16[256,512]{1,0:T(8,128)(2,1)}, bf16[256,512]{1,0:T(8,128)(2,1)}, f32[32,512]{1,0:T(8,128)}, f32[3,512]...) custom-call(f32[8,256,128]{2,1,0:T(8,128)} %get-tuple-element.21.landed, ...), custom_call_target="tpu_custom_call" | custom-call | tf_op jit(solution)/shard_map/finish_outputs/pallas_call | solution.py:891
